TPU v7x, 32 devices: a whole 2x2x4 slice. The times are simulated.
32 devices in a mesh: seq: 2 (over core), dp: 16 (over z, y, x).
Axes of the slice: x: 2, y: 2, z: 4, core: 2. Of those that a mesh axis runs over, the one named last changes fastest.
Arguments:
- hidden: bfloat16 [16, 512, 2560], P('dp', 'seq'), may hold values from -6 to 6
- scan_input: bfloat16 [16, 512, 2560], P('dp', 'seq'), may hold values from -6 to 6
- grad_out: bfloat16 [16, 512, 2560], P('dp', 'seq'), may hold values from -6 to 6
- step_size: float32 [16, 40, 512], P('dp', None, 'seq'), may hold values from 0.5 to 400
- proj_weight: bfloat16 [2560, 256], replicated, may hold values from -0.0068359375 to 0.0068359375
- log_rate: float32 [40], replicated, may hold values from -7.825 to -3.506
- skip_gain: float32 [40], replicated, may hold values from 0.5 to 1.5
- tile_list: int32 [16, 2], P('dp', 'seq'), may hold values from 0 to 1, as said below
Outputs:
- grad_input: bfloat16 [16, 512, 2560], P('dp', 'seq')
- grad_step: float32 [16, 40, 512], P('dp', None, 'seq')
- grad_weight: float32 [2560, 256], P('seq')
- grad_rate: float32 [40], P('seq')
- grad_skip: float32 [40], P('seq')
Inputs may be any that keep to these rules, and one draw needn't show every extreme that they name: `tile_list`: for each device, its 1 entries list the local indices of its valid groups in increasing order, then 1 in every unused entry; in every draw some device has the one group valid.
All inputs are finite; a program needn't handle non-finite values.
Results may differ from a plain program's by a relative error of at most 0.003.
Values sent between devices are 32-bit elements; how exact they have to be, the bound alone decides.
A program may use at most 192 MiB of HBM per device.

v0:
```python
import functools

import jax
import jax.numpy as jnp
from jax import lax
from jax.experimental import pallas as pl
from jax.experimental.pallas import tpu as pltpu
from jax.sharding import PartitionSpec as P

MESH = pl.DeviceIdType.MESH
EXACT = lax.Precision.HIGHEST
F32 = jnp.float32
BF16 = jnp.bfloat16
LOG2E = 1.4426950408889634
PAD = 128
SLAB = 512
VMEM = pl.BlockSpec(memory_space=pltpu.VMEM)
SMEM = pl.BlockSpec(memory_space=pltpu.SMEM)
PARAMS = pltpu.CompilerParams(vmem_limit_bytes=56 * 1024 * 1024)


def dot(a, b, dims=((1,), (0,)), precision=None):
    return lax.dot_general(a, b, (dims, ((), ())), precision=precision, preferred_element_type=F32)


def split(a):
    high = a.astype(BF16)
    return high, (a - high.astype(F32)).astype(BF16)


def to_column(row, count):
    rows = lax.broadcasted_iota(jnp.int32, (count, count), 0)
    cols = lax.broadcasted_iota(jnp.int32, (count, count), 1)
    return jnp.sum(jnp.where(rows == cols, row, 0.0), axis=1, keepdims=True)


def to_row(column, count):
    rows = lax.broadcasted_iota(jnp.int32, (count, PAD), 0)
    cols = lax.broadcasted_iota(jnp.int32, (count, PAD), 1)
    return jnp.sum(jnp.where(rows == cols, column, 0.0), axis=0, keepdims=True)


def head_spread(start, size, width):
    rows = lax.broadcasted_iota(jnp.int32, (PAD, size), 0)
    cols = lax.broadcasted_iota(jnp.int32, (PAD, size), 1) + start
    return jnp.where((cols >= rows * width) & (cols < (rows + 1) * width), 1.0, 0.0).astype(F32)


def pad_rows(a):
    return jnp.concatenate([a, jnp.zeros((PAD - a.shape[0], a.shape[1]), a.dtype)], axis=0)


def prep_kernel(
    heads, width, tile, hidden, weight, x, dy, step, log_rate, proj, tt, zs, alpha_t, l_row, l_col
):
    first = lax.axis_index("seq") == 0
    tokens = hidden.shape[0]
    state = weight.shape[1] // 2
    mask = jnp.where(tile[0, 0] == 0, 1.0, 0.0).astype(F32)
    projected = dot(hidden[...], weight[...])
    proj[...] = projected
    rate = -jnp.exp(to_column(log_rate[...], heads))
    masked = step[...] * mask
    rows = lax.broadcasted_iota(jnp.int32, (tokens, tokens), 0)
    cols = lax.broadcasted_iota(jnp.int32, (tokens, tokens), 1)
    lower = jnp.where(rows <= cols, 1.0, 0.0).astype(F32)
    running = dot(masked * rate, lower, precision=EXACT)
    alpha = jnp.where(first, jnp.exp(running[:, tokens - 1 :] - running) * masked, jnp.exp(running) * mask)
    alpha_cols = pad_rows(alpha).T
    alpha_t[...] = alpha_cols
    l_row[...] = running * LOG2E
    shifted = jnp.where(mask > 0.0, (running - jnp.log(step[...])) * LOG2E, 1e30)
    l_col[...] = pad_rows(shifted).T
    keys = jnp.where(first, projected[:, :state], projected[:, state:])
    both_keys = jnp.concatenate(split(keys), axis=1).T
    alpha_high, alpha_low = split(alpha_cols)
    both_alpha = jnp.concatenate([alpha_high, alpha_low], axis=1)
    for start in range(0, x.shape[1], SLAB):
        at = slice(start, start + SLAB)
        spread = head_spread(start, SLAB, width).astype(BF16)
        wide = dot(both_alpha, jnp.concatenate([spread, spread], axis=0))
        z = jnp.where(first, x[:, at].astype(F32), dy[:, at].astype(F32))
        scaled = (z * wide).astype(BF16)
        zs[:, at] = scaled
        both = dot(both_keys, scaled)
        tt[:, at] = both[:state] + both[state:]


def heads_kernel(heads, width, proj, x, dy, l_row, l_col, qt, dx, r_row, t_col, g):
    tokens = x.shape[0]
    state = proj.shape[1] // 2
    half = tokens // 2
    pair = 2 * width
    g[...] = dot(proj[:, :state], proj[:, state:], ((1,), (1,)), EXACT)
    qt[...] = jnp.zeros_like(qt)
    t_col[...] = jnp.zeros_like(t_col)
    rows = lax.broadcasted_iota(jnp.int32, (half, half), 0)
    cols = lax.broadcasted_iota(jnp.int32, (half, half), 1)
    causal = cols >= rows
    lane = lax.broadcasted_iota(jnp.int32, (1, pair), 1)
    lanes = lax.broadcasted_iota(jnp.int32, (tokens, PAD), 1)
    in_first = lane < width
    keep = [jnp.where(in_first, 1.0, 0.0).astype(BF16), jnp.where(in_first, 0.0, 1.0).astype(BF16)]

    @pl.loop(0, heads // 2)
    def _(k):
        at = pl.ds(pl.multiple_of(k * pair, pair), pair)
        x2 = x[:, at]
        dy2 = dy[:, at]
        columns = pltpu.roll(l_col[...], lax.rem(PAD - 2 * k, PAD), 1)
        sums = t_col[...]
        pieces = []
        for side in range(2):
            head = 2 * k + side
            l_j = columns[:, side : side + 1]
            l_i = l_row[pl.ds(head, 1), :]
            xs = x2 * keep[side]
            w_top = dot(xs[:half], dy2, ((1,), (1,)))
            w_low = dot(xs[half:], dy2[half:], ((1,), (1,)))

            def block(j, i, w, masked):
                js, at_i = slice(j * half, (j + 1) * half), slice(i * half, (i + 1) * half)
                spread = l_i[:, at_i] - l_j[js]
                if masked:
                    spread = jnp.where(causal, spread, -1e30)
                decay = jnp.exp2(spread)
                qt[js, at_i] += decay * w
                mix = decay * g[js, at_i]
                return mix, mix * w

            m00, e00 = block(0, 0, w_top[:, :half], True)
            m01, e01 = block(0, 1, w_top[:, half:], False)
            m11, e11 = block(1, 1, w_low, True)
            r_row[pl.ds(head, 1), :] = jnp.concatenate(
                [jnp.sum(e00, axis=0, keepdims=True), jnp.sum(e01 + e11, axis=0, keepdims=True)], axis=1
            )
            column = jnp.concatenate(
                [jnp.sum(e00 + e01, axis=1, keepdims=True), jnp.sum(e11, axis=1, keepdims=True)], axis=0
            )
            sums = jnp.where(lanes == head, column, sums)
            top = dot(jnp.concatenate([m00.astype(BF16), m01.astype(BF16)], axis=1), dy2)
            low = dot(m11.astype(BF16), dy2[half:])
            pieces.append((top, low))
        t_col[...] = sums
        dx[:half, at] = jnp.where(in_first, pieces[0][0], pieces[1][0])
        dx[half:, at] = jnp.where(in_first, pieces[0][1], pieces[1][1])


def finish_kernel(
    heads, width, tile, rt, proj, zs, alpha_t, qt, dx, r_row, t_col, x, dy, hidden, step, log_rate, gain,
    grad_x, grad_step, grad_w, small,
):
    first = lax.axis_index("seq") == 0
    tokens = x.shape[0]
    state = proj.shape[1] // 2
    mask = jnp.where(tile[0, 0] == 0, 1.0, 0.0).astype(F32)
    on_first = jnp.where(first, 1.0, 0.0).astype(F32)
    keys, query = proj[:, :state], proj[:, state:]
    both_keys = jnp.concatenate(split(jnp.where(first, keys, query)), axis=1)
    alpha_high, alpha_low = split(alpha_t[...] * on_first)
    both_alpha = jnp.concatenate([alpha_high, alpha_low], axis=1)
    gains = jnp.concatenate([gain[...] * mask, jnp.zeros((1, PAD - heads), F32)], axis=1)
    gains = jnp.broadcast_to(gains, (8, PAD))
    carried = jnp.zeros((tokens, PAD), F32)
    skip = jnp.zeros((8, PAD), F32)
    grad_keys = jnp.zeros((tokens, 2 * state), F32)
    for start in range(0, x.shape[1], SLAB):
        at = slice(start, start + SLAB)
        spread = head_spread(start, SLAB, width)
        spread_b = spread.astype(BF16)
        r_high, r_low = split(rt[:, at])
        back = dot(both_keys, jnp.concatenate([r_high, r_high], axis=0))
        scaled = zs[:, at]
        grad_keys += dot(scaled, jnp.concatenate([r_high, r_low], axis=0), ((1,), (1,)))
        p_high, p_low = split(scaled.astype(F32) * back)
        carried += dot(p_high, spread_b, ((1,), (1,))) + dot(p_low, spread_b, ((1,), (1,)))
        wide = dot(both_alpha, jnp.concatenate([spread_b, spread_b], axis=0))
        gain_row = dot(gains, spread, precision=EXACT)[0:1]
        out = dy[:, at].astype(F32)
        grad_x[:, at] = (dx[:, at] + wide * back + gain_row * out).astype(BF16)
        total = jnp.sum(x[:, at].astype(F32) * out, axis=0, keepdims=True)
        skip += dot(jnp.broadcast_to(total, (8, SLAB)), spread, ((1,), (1,)), EXACT)
    grad_keys = grad_keys[:, :state] + grad_keys[:, state:]
    grad_b = dot(qt[...], query, precision=EXACT) + on_first * grad_keys
    grad_c = dot(qt[...], keys, ((0,), (0,)), EXACT) + (1.0 - on_first) * grad_keys
    grad_p = jnp.concatenate([grad_b, grad_c], axis=1).astype(BF16)
    for start in range(0, hidden.shape[1], SLAB):
        grad_w[start : start + SLAB, :] = dot(hidden[:, start : start + SLAB], grad_p, ((0,), (0,)))
    rate = -jnp.exp(to_column(log_rate[...], heads))
    masked = step[...] * mask
    crossing = carried.T[:heads]
    weighted = t_col[...].T[:heads]
    sign = 1.0 - 2.0 * on_first
    grad_l = r_row[...] - weighted + sign * crossing
    rows = lax.broadcasted_iota(jnp.int32, (tokens, tokens), 0)
    cols = lax.broadcasted_iota(jnp.int32, (tokens, tokens), 1)
    upper = jnp.where(rows >= cols, 1.0, 0.0).astype(F32)
    grad_log = dot(grad_l, upper, precision=EXACT)
    grad_log += on_first * jnp.sum(crossing, axis=1, keepdims=True)
    grad_step[...] = mask * ((weighted + on_first * crossing) / step[...] + rate * grad_log)
    grad_rate = jnp.sum(grad_log * masked, axis=1, keepdims=True) * rate
    row = lax.broadcasted_iota(jnp.int32, (8, PAD), 0)
    small[...] = jnp.where(row == 0, to_row(grad_rate, heads), jnp.where(row == 1, skip * mask, 0.0))


def plan(rows, bits, order):
    steps = []
    for bit in order:
        halves = rows % 16 == 0
        rows = rows // 2 if halves else rows
        steps.append((bit, rows, halves))
    return steps


def reduce_kernel(
    bits, scenes, plans, chunk_rows, heads, w, small, out, rate_out, skip_out, acc, sacc, *rest
):
    bufs = rest[: len(plans)]
    sbuf, sems_send, sems_recv = rest[len(plans) :]
    seq, dp = lax.axis_index("seq"), lax.axis_index("dp")
    share = out.shape[0]

    def flipped(bit):
        mine = lax.rem(dp // (1 << bit), 2)
        return mine, dp + (1 - 2 * mine) * (1 << bit)

    other = 1 - seq
    barrier = pltpu.get_barrier_semaphore()
    pl.semaphore_signal(barrier, inc=1, device_id=(other, dp), device_id_type=MESH)
    for bit in range(bits):
        pl.semaphore_signal(barrier, inc=1, device_id=(seq, flipped(bit)[1]), device_id_type=MESH)
    pl.semaphore_wait(barrier, bits + 1)

    count = [0]
    pending = []

    def send(src, dst, target):
        n = count[0]
        count[0] += 1
        copy = pltpu.make_async_remote_copy(
            src_ref=src, dst_ref=dst, send_sem=sems_send.at[n], recv_sem=sems_recv.at[n],
            device_id=target, device_id_type=MESH,
        )
        copy.start()
        pending.append(copy)
        return copy

    def aligned(v):
        return pl.multiple_of(v, 8)

    bases, copies = [], []
    base = 0
    for c, rows in enumerate(chunk_rows):
        bases.append(base)
        copies.append(
            send(w.at[pl.ds(aligned(other * share + base), rows)], bufs[c].at[pl.ds(0, rows)], (other, dp))
        )
        base += rows
    scopy = send(small, sbuf.at[0], (other, dp))

    starts = [None] * len(plans)
    offsets = [0] * len(plans)
    sizes = list(chunk_rows)
    history = [[] for _ in plans]
    for c, rows in enumerate(chunk_rows):
        copies[c].wait_recv()
        mine = w[pl.ds(aligned(seq * share + bases[c]), rows), :]
        acc[pl.ds(bases[c], rows), :] = mine + bufs[c][0:rows, :]
        starts[c] = bases[c]
        offsets[c] = rows
        bit, kept, halves = plans[c][0]
        side, peer = flipped(bit)
        copies[c] = start_step(send, aligned, acc, bufs, c, starts, offsets, bit, kept, halves, side, peer, seq, history)
    scopy.wait_recv()
    sacc[0] = small[...] + sbuf[0]
    scopy = send(sacc.at[0], sbuf.at[1], (seq, flipped(0)[1]))

    for s in range(bits):
        for c in range(len(plans)):
            bit, kept, halves = plans[c][s]
            copies[c].wait_recv()
            if not halves:
                copies[c].wait_send()
                pending[:] = [p for p in pending if p is not copies[c]]
            here = pl.ds(starts[c], kept)
            acc[here, :] = acc[here, :] + bufs[c][offsets[c] - kept : offsets[c], :]
            if s + 1 < bits:
                bit, kept, halves = plans[c][s + 1]
                side, peer = flipped(bit)
                copies[c] = start_step(
                    send, aligned, acc, bufs, c, starts, offsets, bit, kept, halves, side, peer, seq, history
                )
        scopy.wait_recv()
        sacc[s + 1] = sacc[s] + sbuf[s + 1]
        if s + 1 < bits:
            scopy = send(sacc.at[s + 1], sbuf.at[s + 2], (seq, flipped(s + 1)[1]))

    scale = 1.0 / scenes
    gathers = [None] * len(plans)
    trail = [[h for h in history[c] if h[3]] for c in range(len(plans))]
    longest = max(len(t) for t in trail)

    def gather(c, n):
        bit, kept, side, _, start = trail[c][len(trail[c]) - 1 - n]
        peer = flipped(bit)[1]
        region = out.at[pl.ds(start, kept)]
        return send(region, region, (seq, peer))

    for c in range(len(plans)):
        kept = plans[c][-1][1]
        here = pl.ds(starts[c], kept)
        out[here, :] = acc[here, :] * scale
        gathers[c] = gather(c, 0)
    total = sacc[bits] * scale
    total = jnp.where(seq == 0, total, pltpu.roll(total, PAD - heads // 2, 1))
    rate_out[...] = total[0:1, : heads // 2]
    skip_out[...] = total[1:2, : heads // 2]
    for n in range(longest):
        for c in range(len(plans)):
            if n < len(trail[c]):
                gathers[c].wait_recv()
                if n + 1 < len(trail[c]):
                    gathers[c] = gather(c, n + 1)
    for copy in pending:
        copy.wait_send()


def start_step(send, aligned, acc, bufs, c, starts, offsets, bit, kept, halves, side, peer, seq, history):
    begin = starts[c]
    if halves:
        source = aligned(begin + (1 - side) * kept)
        starts[c] = aligned(begin + side * kept)
    else:
        source = begin
    offset = offsets[c]
    offsets[c] = offset + kept
    history[c].append((bit, kept, side, halves, starts[c]))
    return send(acc.at[pl.ds(source, kept)], bufs[c].at[pl.ds(offset, kept)], (seq, peer))


def reduce_all(grad_w, small, scenes, heads):
    seqs = lax.axis_size("seq")
    bits = scenes.bit_length() - 1
    rows = grad_w.shape[0] // seqs
    low = rows // 5
    chunk_rows = (2 * low, 2 * low, rows - 4 * low)
    natural = list(range(bits))
    orders = (natural, [1, 0] + natural[2:], natural[2:] + natural[:2])
    plans = [plan(r, bits, o) for r, o in zip(chunk_rows, orders)]
    scratch = [pltpu.VMEM((rows, grad_w.shape[1]), F32), pltpu.VMEM((bits + 1, 8, PAD), F32)]
    for r, steps in zip(chunk_rows, plans):
        scratch.append(pltpu.VMEM((r + sum(k for _, k, _ in steps), grad_w.shape[1]), F32))
    scratch.append(pltpu.VMEM((bits + 1, 8, PAD), F32))
    copies = len(plans) * (1 + 2 * bits) + bits + 1
    scratch += [pltpu.SemaphoreType.DMA((copies,)), pltpu.SemaphoreType.DMA((copies,))]
    return pl.pallas_call(
        functools.partial(reduce_kernel, bits, scenes, plans, chunk_rows, heads),
        out_shape=(
            jax.ShapeDtypeStruct((rows, grad_w.shape[1]), F32),
            jax.ShapeDtypeStruct((1, heads // seqs), F32),
            jax.ShapeDtypeStruct((1, heads // seqs), F32),
        ),
        in_specs=[VMEM, VMEM],
        out_specs=(VMEM, VMEM, VMEM),
        scratch_shapes=scratch,
        compiler_params=pltpu.CompilerParams(
            collective_id=0, has_side_effects=True, vmem_limit_bytes=40 * 1024 * 1024
        ),
    )(grad_w, small)


def shards(hidden, scan_input, grad_out, step_size, proj_weight, log_rate, skip_gain, tile_list):
    tokens, inner = scan_input.shape[1:]
    model, two_state = proj_weight.shape
    heads = log_rate.shape[0]
    width = inner // heads
    scenes = lax.axis_size("dp")
    x, dy, acts, step = scan_input[0], grad_out[0], hidden[0], step_size[0]
    log_rate, gain = log_rate[None], skip_gain[None]

    def shape(*dims, dtype=F32):
        return jax.ShapeDtypeStruct(dims, dtype)

    proj, tt, zs, alpha_t, l_row, l_col = pl.pallas_call(
        functools.partial(prep_kernel, heads, width),
        out_shape=(
            shape(tokens, two_state), shape(two_state // 2, inner), shape(tokens, inner, dtype=BF16),
            shape(tokens, PAD), shape(heads, tokens), shape(tokens, PAD),
        ),
        in_specs=[SMEM] + [VMEM] * 6,
        out_specs=(VMEM,) * 6,
        compiler_params=PARAMS,
        name="prep",
    )(tile_list, acts, proj_weight, x, dy, step, log_rate)
    rt = lax.ppermute(tt, "seq", [(0, 1), (1, 0)])
    qt, dx, r_row, t_col = pl.pallas_call(
        functools.partial(heads_kernel, heads, width),
        out_shape=(
            shape(tokens, tokens), shape(tokens, inner), shape(heads, tokens), shape(tokens, PAD),
        ),
        in_specs=[VMEM] * 5,
        out_specs=(VMEM,) * 4,
        scratch_shapes=[pltpu.VMEM((tokens, tokens), F32)],
        compiler_params=PARAMS,
        cost_estimate=pl.CostEstimate(flops=8 * 10**9, bytes_accessed=8 * 10**6, transcendentals=3 * 10**6),
        name="heads",
    )(proj, x, dy, l_row, l_col)
    grad_x, grad_step, grad_w, small = pl.pallas_call(
        functools.partial(finish_kernel, heads, width),
        out_shape=(
            shape(tokens, inner, dtype=BF16), shape(heads, tokens), shape(model, two_state), shape(8, PAD),
        ),
        in_specs=[SMEM] + [VMEM] * 14,
        out_specs=(VMEM,) * 4,
        compiler_params=PARAMS,
        name="finish",
    )(tile_list, rt, proj, zs, alpha_t, qt, dx, r_row, t_col, x, dy, acts, step, log_rate, gain)
    summed, rates, gains = reduce_all(grad_w, small, scenes, heads)
    return grad_x[None], grad_step[None], summed, rates[0], gains[0]


def solution(mesh):
    in_specs = (
        P("dp", "seq", None),
        P("dp", "seq", None),
        P("dp", "seq", None),
        P("dp", None, "seq"),
        P(),
        P(),
        P(),
        P("dp", "seq"),
    )
    out_specs = (P("dp", "seq", None), P("dp", None, "seq"), P("seq", None), P("seq"), P("seq"))
    return jax.shard_map(shards, mesh=mesh, in_specs=in_specs, out_specs=out_specs, check_vma=False)
```

profile of v0, /device:TPU:0, one launch (start us, length us, event | category | flops | bytes accessed | tf_op | source)
XLA Modules:
  0.0 84.9 jit_solution(4142922654058626344)
XLA Ops:
  1.3 6.3 %prep.1 = (f32[256,256]{1,0:T(8,128)}, f32[128,2560]{1,0:T(8,128)}, bf16[256,2560]{1,0:T(8,128)(2,1)}, f32[256,128]{1,0:T(8,128)}, f32[40,256]{1,0:T(8,128)}, /*index=5*/f32[256,128]{1,0:T(8,128)}) custom-call(s32[1,1]{1,0:T(1,128)S(6)} %copy.16.tile, bf16[256,2560]{1,0:T(8,128)(2,1)} %bitcast.12, bf16[2560,256]{1,0:T(8,128)(2,1)} %weight.1, ...), custom_call_target="tpu_custom_call" | custom-call | tf_op jit(solution)/shard_map/prep/pallas_call | solution.py:384
  7.5 0.5 collective-permute-start
  8.0 14.4 %heads.1 = (f32[256,256]{1,0:T(8,128)}, f32[256,2560]{1,0:T(8,128)}, f32[40,256]{1,0:T(8,128)}, f32[256,128]{1,0:T(8,128)}) custom-call(f32[256,256]{1,0:T(8,128)} %get-tuple-element.23.proj, bf16[256,2560]{1,0:T(8,128)(2,1)} %bitcast.15, bf16[256,2560]{1,0:T(8,128)(2,1)} %bitcast.18, f32[40,256]{1,0:T(8,128)} %get-tuple-element.26.l_row, ...), custom_call_target="tpu_custom_call" | custom-call | flops 8000000000 | bytes 8000000 | tf_op jit(solution)/shard_map/heads/pallas_call | solution.py:396
  22.4 0.0 collective-permute-done.rt
  22.4 0.0 copy-start.2
  22.4 1.1 %copy-done.2 = f32[128,2560]{1,0:T(8,128)} copy-done((f32[128,2560]{1,0:T(8,128)}, f32[128,2560]{1,0:T(8,128)S(1)}, u32[]{:S(2)}) %copy-start.2) | copy-done | bytes 1310744
  23.5 10.8 %finish.1 = (bf16[256,2560]{1,0:T(8,128)(2,1)}, f32[40,256]{1,0:T(8,128)}, f32[2560,256]{1,0:T(8,128)}, f32[8,128]{1,0:T(8,128)}) custom-call(s32[1,1]{1,0:T(1,128)S(6)} %copy.16.tile, f32[128,2560]{1,0:T(8,128)} %copy-done.2, f32[256,256]{1,0:T(8,128)} %get-tuple-element.23.proj, bf16[256,2560]{1,0:T(8,128)(2,1)} %get-tuple-element.24.zs, ...), custom_call_target="tpu_custom_call" | custom-call | tf_op jit(solution)/shard_map/finish/pallas_call | solution.py:408
  34.2 0.0 copy-start
  34.2 1.7 %copy-done = f32[2560,256]{1,0:T(8,128)S(1)} copy-done((f32[2560,256]{1,0:T(8,128)S(1)}, f32[2560,256]{1,0:T(8,128)}, u32[]{:S(2)}) %copy-start) | copy-done | bytes 2621464
  36.0 0.0 copy-start.1
  36.0 0.7 copy-done.1
  36.7 46.1 %shard_map.119 = (f32[1280,256]{1,0:T(8,128)S(1)}, f32[1,20]{1,0:T(1,128)S(1)}, f32[1,20]{1,0:T(1,128)S(1)}) custom-call(f32[2560,256]{1,0:T(8,128)S(1)} %copy-done, f32[8,128]{1,0:T(8,128)S(1)} %copy-done.1), custom_call_target="tpu_custom_call" | custom-call | tf_op jit(solution)/shard_map/pallas_call | solution.py:356
  82.8 1.1 %copy.17 = f32[1280,256]{1,0:T(8,128)} copy(f32[1280,256]{1,0:T(8,128)S(1)} %get-tuple-element.46) | data formatting | bytes 2621440
  83.9 0.5 copy.18
  84.4 0.5 copy.19
Async XLA Ops:
  7.5 14.9 %collective-permute-start = (f32[128,2560]{1,0:T(8,128)}, f32[128,2560]{1,0:T(8,128)S(1)}, u32[]{:S(2)}, u32[]{:S(2)}) collective-permute-start(f32[128,2560]{1,0:T(8,128)} %get-tuple-element.22), channel_id=1, source_target_pairs={{0,16},{16,0},{1,17},{17,1},{2,18},{18,2},{3,19},{19,3},{4,20},{20... | collective-permute-start | bytes 3932168 | tf_op jit(solution)/shard_map/ppermute | solution.py:395
  22.4 1.1 %copy-start.2 = (f32[128,2560]{1,0:T(8,128)}, f32[128,2560]{1,0:T(8,128)S(1)}, u32[]{:S(2)}) copy-start(f32[128,2560]{1,0:T(8,128)S(1)} %collective-permute-done.rt) | copy-start | bytes 3932164
  34.2 1.7 %copy-start = (f32[2560,256]{1,0:T(8,128)S(1)}, f32[2560,256]{1,0:T(8,128)}, u32[]{:S(2)}) copy-start(f32[2560,256]{1,0:T(8,128)} %get-tuple-element.34.w) | copy-start | bytes 7864324
  36.0 0.7 copy-start.1
where the time goes:
time: 85.1 us; the launch traced here: 84.9 us
  Pallas kernels  77.6 us (91%)
  local copies, waits for them, and re-layouts  5.55 us (7%)
  between operations  1.3 us (2%)
    pallas_call x1, Pallas kernels, reduce_all(): pl.pallas_call(functools.partial(reduce_kernel, bits, scenes, plans, chun...  46.1 us
    pallas_call x1, Pallas kernels, shards(): pl.pallas_call(functools.partial(heads_kernel, heads, width), out_shape=(...  14.4 us
    pallas_call x1, Pallas kernels, shards(): pl.pallas_call(functools.partial(finish_kernel, heads, width), out_shape=...  10.8 us
    pallas_call x1, Pallas kernels, shards(): pl.pallas_call(functools.partial(prep_kernel, heads, width), out_shape=(s...  6.26 us
    unnamed x9, local copies, waits for them, and re-layouts  5.55 us
  transfers between devices with their start and end apart: 1, of which 0 were waited for; matrix products, arithmetic and copies ran while one was open for 0% of the time, Pallas kernels for 17%

commit v1 on v0

v1 whole, which is shorter than its diff:
```python
import functools

import jax
import jax.numpy as jnp
from jax import lax
from jax.experimental import pallas as pl
from jax.experimental.pallas import tpu as pltpu
from jax.sharding import PartitionSpec as P

MESH = pl.DeviceIdType.MESH
EXACT = lax.Precision.HIGHEST
F32 = jnp.float32
BF16 = jnp.bfloat16
LOG2E = 1.4426950408889634
PAD = 128
SLAB = 512
ORDER = (2, 0, 1)
QUOTAS = (3, 4, 1, 3, 2, 1, 3, 1, 1, 1, 1, 1, 2, 2, 1)
VMEM = pl.BlockSpec(memory_space=pltpu.VMEM)
SMEM = pl.BlockSpec(memory_space=pltpu.SMEM)
PARAMS = pltpu.CompilerParams(vmem_limit_bytes=56 * 1024 * 1024)


def dot(a, b, dims=((1,), (0,)), precision=None):
    return lax.dot_general(a, b, (dims, ((), ())), precision=precision, preferred_element_type=F32)


def split(a):
    high = a.astype(BF16)
    return high, (a - high.astype(F32)).astype(BF16)


def to_column(row, count):
    rows = lax.broadcasted_iota(jnp.int32, (count, count), 0)
    cols = lax.broadcasted_iota(jnp.int32, (count, count), 1)
    return jnp.sum(jnp.where(rows == cols, row, 0.0), axis=1, keepdims=True)


def to_row(column, count):
    rows = lax.broadcasted_iota(jnp.int32, (count, PAD), 0)
    cols = lax.broadcasted_iota(jnp.int32, (count, PAD), 1)
    return jnp.sum(jnp.where(rows == cols, column, 0.0), axis=0, keepdims=True)


def head_spread(start, size, width):
    rows = lax.broadcasted_iota(jnp.int32, (PAD, size), 0)
    cols = lax.broadcasted_iota(jnp.int32, (PAD, size), 1) + start
    return jnp.where((cols >= rows * width) & (cols < (rows + 1) * width), 1.0, 0.0).astype(F32)


def pad_rows(a):
    return jnp.concatenate([a, jnp.zeros((PAD - a.shape[0], a.shape[1]), a.dtype)], axis=0)


def prep_kernel(
    heads, width, tile, hidden, weight, x, dy, step, log_rate, proj, tt, zs, alpha_t, l_row, l_col
):
    first = lax.axis_index("seq") == 0
    tokens = hidden.shape[0]
    state = weight.shape[1] // 2
    mask = jnp.where(tile[0, 0] == 0, 1.0, 0.0).astype(F32)
    projected = dot(hidden[...], weight[...])
    proj[...] = projected
    rate = -jnp.exp(to_column(log_rate[...], heads))
    masked = step[...] * mask
    rows = lax.broadcasted_iota(jnp.int32, (tokens, tokens), 0)
    cols = lax.broadcasted_iota(jnp.int32, (tokens, tokens), 1)
    lower = jnp.where(rows <= cols, 1.0, 0.0).astype(F32)
    running = dot(masked * rate, lower, precision=EXACT)
    alpha = jnp.where(first, jnp.exp(running[:, tokens - 1 :] - running) * masked, jnp.exp(running) * mask)
    alpha_cols = pad_rows(alpha).T
    alpha_t[...] = alpha_cols
    l_row[...] = running * LOG2E
    shifted = jnp.where(mask > 0.0, (running - jnp.log(step[...])) * LOG2E, 1e30)
    l_col[...] = pad_rows(shifted).T
    keys = jnp.where(first, projected[:, :state], projected[:, state:])
    both_keys = jnp.concatenate(split(keys), axis=1).T
    alpha_high, alpha_low = split(alpha_cols)
    both_alpha = jnp.concatenate([alpha_high, alpha_low], axis=1)
    for start in range(0, x.shape[1], SLAB):
        at = slice(start, start + SLAB)
        spread = head_spread(start, SLAB, width).astype(BF16)
        wide = dot(both_alpha, jnp.concatenate([spread, spread], axis=0))
        z = jnp.where(first, x[:, at].astype(F32), dy[:, at].astype(F32))
        scaled, scaled_low = split(z * wide)
        zs[:, at] = scaled
        both = dot(both_keys, scaled) + dot(both_keys, scaled_low)
        tt[:, at] = both[:state] + both[state:]


def pair_parts(k, heads, width, x, dy, l_row, l_col):
    tokens = x.shape[0]
    half = tokens // 2
    pair = 2 * width
    rows = lax.broadcasted_iota(jnp.int32, (half, half), 0)
    cols = lax.broadcasted_iota(jnp.int32, (half, half), 1)
    causal = cols >= rows
    in_first = lax.broadcasted_iota(jnp.int32, (1, pair), 1) < width
    keep = [jnp.where(in_first, 1.0, 0.0).astype(BF16), jnp.where(in_first, 0.0, 1.0).astype(BF16)]
    at = pl.ds(pl.multiple_of(k * pair, pair), pair)
    x2 = x[:, at]
    dy2 = dy[:, at]
    columns = pltpu.roll(l_col[...], lax.rem(PAD - 2 * k, PAD), 1)
    sides = []
    for side in range(2):
        l_j = columns[:, side : side + 1]
        l_i = l_row[pl.ds(2 * k + side, 1), :]
        xs = x2 * keep[side]
        w_top = dot(xs[:half], dy2, ((1,), (1,)))
        w_low = dot(xs[half:], dy2[half:], ((1,), (1,)))
        d00 = jnp.exp2(jnp.where(causal, l_i[:, :half] - l_j[:half], -1e30))
        d01 = jnp.exp2(l_i[:, half:] - l_j[:half])
        d11 = jnp.exp2(jnp.where(causal, l_i[:, half:] - l_j[half:], -1e30))
        sides.append(((d00, w_top[:, :half]), (d01, w_top[:, half:]), (d11, w_low)))
    return at, dy2, in_first, sides


def heads_kernel(heads, width, x, dy, l_row, l_col, qt):
    half = x.shape[0] // 2
    qt[...] = jnp.zeros_like(qt)

    @pl.loop(0, heads // 2)
    def _(k):
        _, _, _, sides = pair_parts(k, heads, width, x, dy, l_row, l_col)
        for n, (j, i) in enumerate(((0, 0), (0, 1), (1, 1))):
            js, at_i = slice(j * half, (j + 1) * half), slice(i * half, (i + 1) * half)
            (d_a, w_a), (d_b, w_b) = sides[0][n], sides[1][n]
            qt[js, at_i] += d_a * w_a + d_b * w_b


def one_pair(k, heads, width, x, dy, l_row, l_col, g, dx, r_row, t_col):
    tokens = x.shape[0]
    half = tokens // 2
    lanes = lax.broadcasted_iota(jnp.int32, (tokens, PAD), 1)
    at, dy2, in_first, sides = pair_parts(k, heads, width, x, dy, l_row, l_col)
    sums = t_col[...]
    pieces = []
    for side in range(2):
        head = 2 * k + side
        (d00, w00), (d01, w01), (d11, w11) = sides[side]
        m00, m01, m11 = d00 * g[:half, :half], d01 * g[:half, half:], d11 * g[half:, half:]
        e00, e01, e11 = m00 * w00, m01 * w01, m11 * w11
        r_row[pl.ds(head, 1), :] = jnp.concatenate(
            [jnp.sum(e00, axis=0, keepdims=True), jnp.sum(e01 + e11, axis=0, keepdims=True)], axis=1
        )
        column = jnp.concatenate(
            [jnp.sum(e00 + e01, axis=1, keepdims=True), jnp.sum(e11, axis=1, keepdims=True)], axis=0
        )
        sums = jnp.where(lanes == head, column, sums)
        top_high, top_low = split(jnp.concatenate([m00, m01], axis=1))
        low_high, low_low = split(m11)
        top = dot(top_high, dy2) + dot(top_low, dy2)
        low = dot(low_high, dy2[half:]) + dot(low_low, dy2[half:])
        pieces.append((top, low))
    t_col[...] = sums
    dx[:half, at] = jnp.where(in_first, pieces[0][0], pieces[1][0])
    dx[half:, at] = jnp.where(in_first, pieces[0][1], pieces[1][1])


def plan(rows, bits, order):
    steps = []
    for bit in order:
        halves = rows % 16 == 0
        rows = rows // 2 if halves else rows
        steps.append((bit, rows, halves))
    return steps


def reduce_kernel(
    bits, scenes, plans, chunk_rows, heads, width,
    tile, rt, proj, zs, alpha_t, qt, hidden, l_row, l_col, step, log_rate, gain, x_hbm, dy_hbm,
    grad_x, grad_step, out, rate_out, skip_out,
    x, dy, dx, r_row, t_col, g, w, small, acc, sacc, *rest
):
    bufs = rest[: len(plans)]
    sbuf, sems_send, sems_recv, sems_load = rest[len(plans) :]
    seq, dp = lax.axis_index("seq"), lax.axis_index("dp")
    share = out.shape[0]
    tokens = x.shape[0]
    state = proj.shape[1] // 2

    def flipped(bit):
        mine = lax.rem(dp // (1 << bit), 2)
        return mine, dp + (1 - 2 * mine) * (1 << bit)

    other = 1 - seq
    loads = [
        pltpu.make_async_copy(x_hbm, x, sems_load.at[0]),
        pltpu.make_async_copy(dy_hbm, dy, sems_load.at[1]),
    ]
    for load in loads:
        load.start()
    barrier = pltpu.get_barrier_semaphore()
    pl.semaphore_signal(barrier, inc=1, device_id=(other, dp), device_id_type=MESH)
    for bit in range(bits):
        pl.semaphore_signal(barrier, inc=1, device_id=(seq, flipped(bit)[1]), device_id_type=MESH)

    mask = jnp.where(tile[0, 0] == 0, 1.0, 0.0).astype(F32)
    on_first = jnp.where(seq == 0, 1.0, 0.0).astype(F32)
    keys, query = proj[:, :state], proj[:, state:]
    grad_keys = jnp.zeros((tokens, 2 * state), F32)
    for start in range(0, zs.shape[1], SLAB):
        at = slice(start, start + SLAB)
        grad_keys += dot(zs[:, at], jnp.concatenate(split(rt[:, at]), axis=0), ((1,), (1,)))
    grad_keys = grad_keys[:, :state] + grad_keys[:, state:]
    grad_b = dot(qt[...], query, precision=EXACT) + on_first * grad_keys
    grad_c = dot(qt[...], keys, ((0,), (0,)), EXACT) + (1.0 - on_first) * grad_keys
    grad_p = jnp.concatenate([grad_b, grad_c], axis=1).astype(BF16)

    count = [0]
    pending = []

    def send(src, dst, target):
        n = count[0]
        count[0] += 1
        copy = pltpu.make_async_remote_copy(
            src_ref=src, dst_ref=dst, send_sem=sems_send.at[n], recv_sem=sems_recv.at[n],
            device_id=target, device_id_type=MESH,
        )
        copy.start()
        pending.append(copy)
        return copy

    def aligned(v):
        return pl.multiple_of(v, 8)

    def weight_rows(start, rows):
        w[pl.ds(aligned(start), rows), :] = dot(
            hidden[:, pl.ds(pl.multiple_of(start, PAD), rows)], grad_p, ((0,), (0,))
        )

    chunks = ORDER
    bases = [sum(chunk_rows[:c]) for c in range(len(plans))]
    copies = [None] * len(plans)
    for n, c in enumerate(chunks):
        rows = chunk_rows[c]
        weight_rows(other * share + bases[c], rows)
        if n == 0:
            pl.semaphore_wait(barrier, bits + 1)
        copies[c] = send(
            w.at[pl.ds(aligned(other * share + bases[c]), rows)], bufs[c].at[pl.ds(0, rows)], (other, dp)
        )

    pair_args = (heads, width, x, dy, l_row, l_col, g, dx, r_row, t_col)
    scale = 1.0 / scenes
    done_pairs = [0]
    done_slabs = [0]
    slabs = zs.shape[1] // SLAB
    terms = {"carried": jnp.zeros((tokens, PAD), F32), "skip": jnp.zeros((8, PAD), F32)}
    light = [-1, None]

    def run_pairs(n):
        lo = done_pairs[0]
        hi = min(lo + n, heads // 2)
        done_pairs[0] = hi
        if lo == 0 and hi > 0:
            g[...] = dot(keys, query, ((1,), (1,)), EXACT)
            t_col[...] = jnp.zeros_like(t_col)
            for load in loads:
                load.wait()
        if hi > lo:

            @pl.loop(lo, hi)
            def _(k):
                one_pair(k, *pair_args)

    def run_slabs(n):
        both_keys = jnp.concatenate(split(jnp.where(seq == 0, keys, query)), axis=1)
        alpha_high, alpha_low = split(alpha_t[...] * on_first)
        both_alpha = jnp.concatenate([alpha_high, alpha_low], axis=1)
        gains = jnp.concatenate([gain[...] * mask, jnp.zeros((1, PAD - heads), F32)], axis=1)
        gains = jnp.broadcast_to(gains, (8, PAD))
        for _ in range(n):
            if done_slabs[0] >= slabs:
                return
            start = done_slabs[0] * SLAB
            done_slabs[0] += 1
            at = slice(start, start + SLAB)
            spread = head_spread(start, SLAB, width)
            spread_b = spread.astype(BF16)
            r_high, r_low = split(rt[:, at])
            back = dot(both_keys, jnp.concatenate([r_high, r_high], axis=0)) + dot(both_keys[:, :state], r_low)
            p_high, p_low = split(zs[:, at].astype(F32) * back)
            terms["carried"] += dot(p_high, spread_b, ((1,), (1,))) + dot(p_low, spread_b, ((1,), (1,)))
            wide = dot(both_alpha, jnp.concatenate([spread_b, spread_b], axis=0))
            gain_row = dot(gains, spread, precision=EXACT)[0:1]
            top = dy[:, at].astype(F32)
            grad_x[:, at] = (dx[:, at] + wide * back + gain_row * top).astype(BF16)
            total = jnp.sum(x[:, at].astype(F32) * top, axis=0, keepdims=True)
            terms["skip"] += dot(jnp.broadcast_to(total, (8, SLAB)), spread, ((1,), (1,)), EXACT)

    def run_last():
        rate = -jnp.exp(to_column(log_rate[...], heads))
        crossing = terms["carried"].T[:heads]
        weighted = t_col[...].T[:heads]
        sign = 1.0 - 2.0 * on_first
        grad_l = r_row[...] - weighted + sign * crossing
        rows = lax.broadcasted_iota(jnp.int32, (tokens, tokens), 0)
        cols = lax.broadcasted_iota(jnp.int32, (tokens, tokens), 1)
        upper = jnp.where(rows >= cols, 1.0, 0.0).astype(F32)
        grad_log = dot(grad_l, upper, precision=EXACT)
        grad_log += on_first * jnp.sum(crossing, axis=1, keepdims=True)
        grad_step[...] = mask * ((weighted + on_first * crossing) / step[...] + rate * grad_log)
        grad_rate = jnp.sum(grad_log * (step[...] * mask), axis=1, keepdims=True) * rate
        row = lax.broadcasted_iota(jnp.int32, (8, PAD), 0)
        small[...] = jnp.where(row == 0, to_row(grad_rate, heads), jnp.where(row == 1, terms["skip"] * mask, 0.0))

    def advance_small():
        stage = light[0]
        if stage > bits:
            return
        if stage >= 0:
            light[1].wait_recv()
            sacc[stage] = (small[...] if stage == 0 else sacc[stage - 1]) + sbuf[stage]
        light[0] = stage = stage + 1
        if stage == 0:
            light[1] = send(small, sbuf.at[0], (other, dp))
        elif stage <= bits:
            light[1] = send(sacc.at[stage - 1], sbuf.at[stage], (seq, flipped(stage - 1)[1]))

    quotas = list(QUOTAS)

    def tick():
        n = quotas.pop(0) if quotas else 1
        if done_pairs[0] < heads // 2:
            run_pairs(n)
        elif done_slabs[0] < slabs:
            run_slabs(n)
            if done_slabs[0] == slabs:
                run_last()
                advance_small()
        else:
            advance_small()

    starts = list(bases)
    offsets = list(chunk_rows)
    history = [[] for _ in plans]

    def start_step(c, s):
        bit, kept, halves = plans[c][s]
        side, peer = flipped(bit)
        begin = starts[c]
        source = begin
        if halves:
            source = aligned(begin + (1 - side) * kept)
            starts[c] = aligned(begin + side * kept)
        offset = offsets[c]
        offsets[c] = offset + kept
        history[c].append((bit, kept, halves, starts[c]))
        copies[c] = send(acc.at[pl.ds(source, kept)], bufs[c].at[pl.ds(offset, kept)], (seq, peer))

    for c in chunks:
        weight_rows(seq * share + bases[c], chunk_rows[c])
    for c in chunks:
        rows = chunk_rows[c]
        copies[c].wait_recv()
        mine = w[pl.ds(aligned(seq * share + bases[c]), rows), :]
        acc[pl.ds(bases[c], rows), :] = mine + bufs[c][0:rows, :]
        start_step(c, 0)

    for s in range(bits):
        for c in chunks:
            tick()
            kept, halves = plans[c][s][1:]
            copies[c].wait_recv()
            if not halves:
                copies[c].wait_send()
                pending[:] = [p for p in pending if p is not copies[c]]
            here = pl.ds(starts[c], kept)
            acc[here, :] = acc[here, :] + bufs[c][offsets[c] - kept : offsets[c], :]
            if s + 1 < bits:
                start_step(c, s + 1)
            else:
                out[here, :] = acc[here, :] * scale

    trail = [[h for h in reversed(history[c]) if h[2]] for c in range(len(plans))]

    def gather(c, n):
        bit, kept, _, start = trail[c][n]
        region = out.at[pl.ds(start, kept)]
        return send(region, region, (seq, flipped(bit)[1]))

    for c in chunks:
        copies[c] = gather(c, 0)
    for n in range(max(len(t) for t in trail)):
        for c in chunks:
            if n < len(trail[c]):
                tick()
                copies[c].wait_recv()
                if n + 1 < len(trail[c]):
                    copies[c] = gather(c, n + 1)
    while light[0] <= bits:
        tick()
    total = sacc[bits] * scale
    total = jnp.where(seq == 0, total, pltpu.roll(total, PAD - heads // 2, 1))
    rate_out[...] = total[0:1, : heads // 2]
    skip_out[...] = total[1:2, : heads // 2]
    for copy in pending:
        copy.wait_send()


def reduce_all(scenes, heads, width, args):
    rt, hidden = args[1], args[6]
    tokens, model = hidden.shape
    inner = rt.shape[1]
    two_state = 2 * rt.shape[0]
    seqs = lax.axis_size("seq")
    bits = scenes.bit_length() - 1
    rows = model // seqs
    low = rows // 5
    chunk_rows = (2 * low, 2 * low, rows - 4 * low)
    natural = list(range(bits))
    orders = (natural, [1, 0] + natural[2:], natural[2:] + natural[:2])
    plans = [plan(r, bits, o) for r, o in zip(chunk_rows, orders)]
    scratch = [
        pltpu.VMEM((tokens, inner), BF16), pltpu.VMEM((tokens, inner), BF16), pltpu.VMEM((tokens, inner), F32),
        pltpu.VMEM((heads, tokens), F32), pltpu.VMEM((tokens, PAD), F32), pltpu.VMEM((tokens, tokens), F32),
        pltpu.VMEM((model, two_state), F32), pltpu.VMEM((8, PAD), F32),
        pltpu.VMEM((rows, two_state), F32), pltpu.VMEM((bits + 1, 8, PAD), F32),
    ]
    for r, steps in zip(chunk_rows, plans):
        scratch.append(pltpu.VMEM((r + sum(k for _, k, _ in steps), two_state), F32))
    scratch.append(pltpu.VMEM((bits + 1, 8, PAD), F32))
    copies = len(plans) * (1 + 2 * bits) + bits + 1
    scratch += [pltpu.SemaphoreType.DMA((copies,)), pltpu.SemaphoreType.DMA((copies,)), pltpu.SemaphoreType.DMA((2,))]
    return pl.pallas_call(
        functools.partial(reduce_kernel, bits, scenes, plans, chunk_rows, heads, width),
        out_shape=(
            jax.ShapeDtypeStruct((tokens, inner), BF16),
            jax.ShapeDtypeStruct((heads, tokens), F32),
            jax.ShapeDtypeStruct((rows, two_state), F32),
            jax.ShapeDtypeStruct((1, heads // seqs), F32),
            jax.ShapeDtypeStruct((1, heads // seqs), F32),
        ),
        in_specs=[SMEM] + [VMEM] * 11 + [pl.BlockSpec(memory_space=pl.ANY)] * 2,
        out_specs=(VMEM,) * 5,
        scratch_shapes=scratch,
        compiler_params=pltpu.CompilerParams(
            collective_id=0, has_side_effects=True, vmem_limit_bytes=48 * 1024 * 1024
        ),
        name="finish",
    )(*args)


def shards(hidden, scan_input, grad_out, step_size, proj_weight, log_rate, skip_gain, tile_list):
    tokens, inner = scan_input.shape[1:]
    model, two_state = proj_weight.shape
    heads = log_rate.shape[0]
    width = inner // heads
    scenes = lax.axis_size("dp")
    x, dy, acts, step = scan_input[0], grad_out[0], hidden[0], step_size[0]
    log_rate, gain = log_rate[None], skip_gain[None]

    def shape(*dims, dtype=F32):
        return jax.ShapeDtypeStruct(dims, dtype)

    proj, tt, zs, alpha_t, l_row, l_col = pl.pallas_call(
        functools.partial(prep_kernel, heads, width),
        out_shape=(
            shape(tokens, two_state), shape(two_state // 2, inner), shape(tokens, inner, dtype=BF16),
            shape(tokens, PAD), shape(heads, tokens), shape(tokens, PAD),
        ),
        in_specs=[SMEM] + [VMEM] * 6,
        out_specs=(VMEM,) * 6,
        compiler_params=PARAMS,
        name="prep",
    )(tile_list, acts, proj_weight, x, dy, step, log_rate)
    rt = lax.ppermute(tt, "seq", [(0, 1), (1, 0)])
    qt = pl.pallas_call(
        functools.partial(heads_kernel, heads, width),
        out_shape=shape(tokens, tokens),
        in_specs=[VMEM] * 4,
        out_specs=VMEM,
        compiler_params=PARAMS,
        cost_estimate=pl.CostEstimate(flops=8 * 10**9, bytes_accessed=8 * 10**6, transcendentals=3 * 10**6),
        name="heads",
    )(x, dy, l_row, l_col)
    args = (tile_list, rt, proj, zs, alpha_t, qt, acts, l_row, l_col, step, log_rate, gain, x, dy)
    grad_x, grad_step, summed, rates, gains = reduce_all(scenes, heads, width, args)
    return grad_x[None], grad_step[None], summed, rates[0], gains[0]


def solution(mesh):
    in_specs = (
        P("dp", "seq", None),
        P("dp", "seq", None),
        P("dp", "seq", None),
        P("dp", None, "seq"),
        P(),
        P(),
        P(),
        P("dp", "seq"),
    )
    out_specs = (P("dp", "seq", None), P("dp", None, "seq"), P("seq", None), P("seq"), P("seq"))
    return jax.shard_map(shards, mesh=mesh, in_specs=in_specs, out_specs=out_specs, check_vma=False)
```

time: 85.1 us -> 72.4 us (0.85)
  Pallas kernels: 77.6 us -> 65.6 us
    pallas_call x2 -> x1, Pallas kernels: 25.2 us -> 7.65 us  [shards(): pl.pallas_call(functools.partial(heads_kernel, heads, width), out_shape=s...]
    pallas_call x1, Pallas kernels: 46.1 us -> 51.4 us  [reduce_all(): pl.pallas_call(functools.partial(reduce_kernel, bits, scenes, plans, chun...]
    unnamed x9 -> x23, local copies, waits for them, and re-layouts: 5.55 us -> 4.73 us
  transfers between devices with their start and end apart: 1 -> 1, of which waited for: 0 -> 0; matrix products, arithmetic and copies ran while one was open for 0% -> 0% of each run, Pallas kernels for 17% -> 11%
where the time goes in v1:
time: 72.4 us; the launch traced here: 72.2 us
  Pallas kernels  65.6 us (91%)
  local copies, waits for them, and re-layouts  4.73 us (7%)
  between operations  1.39 us (2%)
    pallas_call x1, Pallas kernels, reduce_all(): pl.pallas_call(functools.partial(reduce_kernel, bits, scenes, plans, chun...  51.4 us
    pallas_call x1, Pallas kernels, shards(): pl.pallas_call(functools.partial(heads_kernel, heads, width), out_shape=s...  7.65 us
    pallas_call x1, Pallas kernels, shards(): pl.pallas_call(functools.partial(prep_kernel, heads, width), out_shape=(s...  6.59 us
    unnamed x23, local copies, waits for them, and re-layouts  4.73 us
  transfers between devices with their start and end apart: 1, of which 0 were waited for; matrix products, arithmetic and copies ran while one was open for 0% of the time, Pallas kernels for 11%

profile of v1, /device:TPU:0, one launch (start us, length us, event | category | flops | bytes accessed | tf_op | source)
XLA Modules:
  0.0 72.2 jit_solution(16715293781147757890)
XLA Ops:
  1.3 6.6 %prep.1 = (f32[256,256]{1,0:T(8,128)}, f32[128,2560]{1,0:T(8,128)}, bf16[256,2560]{1,0:T(8,128)(2,1)}, f32[256,128]{1,0:T(8,128)}, f32[40,256]{1,0:T(8,128)}, /*index=5*/f32[256,128]{1,0:T(8,128)}) custom-call(s32[1,1]{1,0:T(1,128)S(6)} %copy.18.tile, bf16[256,2560]{1,0:T(8,128)(2,1)} %bitcast.19, bf16[2560,256]{1,0:T(8,128)(2,1)} %weight.1, ...), custom_call_target="tpu_custom_call" | custom-call | tf_op jit(solution)/shard_map/prep/pallas_call | solution.py:457
  7.9 0.5 collective-permute-start
  8.3 0.0 copy-start
  8.3 0.0 copy-start.1
  8.3 0.0 copy-start.3
  8.3 0.0 copy-start.4
  8.3 0.0 copy-start.5
  8.3 0.0 copy-start.6
  8.3 0.0 copy-start.7
  8.4 0.0 copy-start.8
  8.4 7.7 %heads.1.qt = f32[256,256]{1,0:T(8,128)} custom-call(bf16[256,2560]{1,0:T(8,128)(2,1)} %bitcast.22, bf16[256,2560]{1,0:T(8,128)(2,1)} %bitcast.25, f32[40,256]{1,0:T(8,128)} %get-tuple-element.20.l_row, f32[256,128]{1,0:T(8,128)} %get-tuple-element.21.l_col), custom_call_target="tpu_custom_call" | custom-call | flops 8000000000 | bytes 8000000 | tf_op jit(solution)/shard_map/heads/pallas_call | solution.py:469
  16.0 0.0 collective-permute-done.rt
  16.0 0.0 copy-done
  16.0 0.0 copy-done.1
  16.0 0.0 copy-done.3
  16.0 0.0 copy-done.4
  16.1 0.0 copy-done.5
  16.1 0.0 copy-done.6
  16.1 0.0 copy-done.7
  16.1 0.0 copy-done.8
  16.1 0.0 copy-start.2
  16.1 0.9 %copy-done.2 = f32[256,256]{1,0:T(8,128)S(1)} copy-done((f32[256,256]{1,0:T(8,128)S(1)}, f32[256,256]{1,0:T(8,128)}, u32[]{:S(2)}) %copy-start.2) | copy-done | bytes 262168
  17.0 51.4 %finish.1 = (bf16[256,2560]{1,0:T(8,128)(2,1)S(1)}, f32[40,256]{1,0:T(8,128)S(1)}, f32[1280,256]{1,0:T(8,128)S(1)}, f32[1,20]{1,0:T(1,128)S(1)}, f32[1,20]{1,0:T(1,128)S(1)}) custom-call(s32[1,1]{1,0:T(1,128)S(6)} %copy.18.tile, f32[128,2560]{1,0:T(8,128)S(1)} %collective-permute-done.rt, f32[256,256]{1,0:T(8,128)S(1)} %copy-done.1, ...), custom_call_target="tpu_custom_call" | custom-call | tf_op jit(solution)/shard_map/finish/pallas_call | solution.py:426
  68.4 1.1 %copy.19 = bf16[1,256,2560]{2,1,0:T(8,128)(2,1)} copy(bf16[1,256,2560]{2,1,0:T(8,128)(2,1)S(1)} %bitcast.10) | data formatting | bytes 2621440
  69.5 0.6 copy.20
  70.1 1.1 %copy.21 = f32[1280,256]{1,0:T(8,128)} copy(f32[1280,256]{1,0:T(8,128)S(1)} %get-tuple-element.34) | data formatting | bytes 2621440
  71.2 0.5 copy.22
  71.7 0.5 copy.23
Async XLA Ops:
  7.9 8.2 %collective-permute-start = (f32[128,2560]{1,0:T(8,128)}, f32[128,2560]{1,0:T(8,128)S(1)}, u32[]{:S(2)}, u32[]{:S(2)}) collective-permute-start(f32[128,2560]{1,0:T(8,128)} %get-tuple-element.16), channel_id=1, source_target_pairs={{0,16},{16,0},{1,17},{17,1},{2,18},{18,2},{3,19},{19,3},{4,20},{20... | collective-permute-start | bytes 3932168 | tf_op jit(solution)/shard_map/ppermute | solution.py:468
  8.3 7.7 %copy-start = (bf16[256,2560]{1,0:T(8,128)(2,1)S(1)}, bf16[256,2560]{1,0:T(8,128)(2,1)}, u32[]{:S(2)}) copy-start(bf16[256,2560]{1,0:T(8,128)(2,1)} %get-tuple-element.18.zs) | copy-start | bytes 3932164
  8.3 7.7 %copy-start.1 = (f32[256,256]{1,0:T(8,128)S(1)}, f32[256,256]{1,0:T(8,128)}, u32[]{:S(2)}) copy-start(f32[256,256]{1,0:T(8,128)} %get-tuple-element.17.proj) | copy-start | bytes 786436
  8.3 7.7 %copy-start.3 = (f32[1,40,256]{2,1,0:T(8,128)S(1)}, f32[1,40,256]{2,1,0:T(8,128)}, u32[]{:S(2)}) copy-start(f32[1,40,256]{2,1,0:T(8,128)} %param.11) | copy-start | bytes 122884
  8.3 7.7 %copy-start.4 = (f32[256,128]{1,0:T(8,128)S(1)}, f32[256,128]{1,0:T(8,128)}, u32[]{:S(2)}) copy-start(f32[256,128]{1,0:T(8,128)} %get-tuple-element.19.alpha_t) | copy-start | bytes 393220
  8.3 7.7 %copy-start.5 = (f32[256,128]{1,0:T(8,128)S(1)}, f32[256,128]{1,0:T(8,128)}, u32[]{:S(2)}) copy-start(f32[256,128]{1,0:T(8,128)} %get-tuple-element.21.l_col) | copy-start | bytes 393220
  8.3 7.7 %copy-start.6 = (f32[40,256]{1,0:T(8,128)S(1)}, f32[40,256]{1,0:T(8,128)}, u32[]{:S(2)}) copy-start(f32[40,256]{1,0:T(8,128)} %get-tuple-element.20.l_row) | copy-start | bytes 122884
  8.3 7.7 %copy-start.7 = (f32[40]{0:T(128)S(1)}, f32[40]{0:T(128)}, u32[]{:S(2)}) copy-start(f32[40]{0:T(128)} %param.13) | copy-start | bytes 484
  8.4 7.7 %copy-start.8 = (f32[40]{0:T(128)S(1)}, f32[40]{0:T(128)}, u32[]{:S(2)}) copy-start(f32[40]{0:T(128)} %param.14) | copy-start | bytes 484
  16.1 1.0 %copy-start.2 = (f32[256,256]{1,0:T(8,128)S(1)}, f32[256,256]{1,0:T(8,128)}, u32[]{:S(2)}) copy-start(f32[256,256]{1,0:T(8,128)} %heads.1.qt) | copy-start | bytes 786436

commit v2 on v1

v2 whole, which is shorter than its diff:
```python
import functools

import jax
import jax.numpy as jnp
from jax import lax
from jax.experimental import pallas as pl
from jax.experimental.pallas import tpu as pltpu
from jax.sharding import PartitionSpec as P

MESH = pl.DeviceIdType.MESH
EXACT = lax.Precision.HIGHEST
F32 = jnp.float32
BF16 = jnp.bfloat16
LOG2E = 1.4426950408889634
PAD = 128
SLAB = 512
QUOTAS = (1, 5, 1, 0, 2, 1, 0, 1, 1, 0, 3, 1, 0, 2, 1, 1, 3, 2, 1, 0, 1, 1, 1, 1, 1)
VMEM = pl.BlockSpec(memory_space=pltpu.VMEM)
SMEM = pl.BlockSpec(memory_space=pltpu.SMEM)


def dot(a, b, dims=((1,), (0,)), precision=None):
    return lax.dot_general(a, b, (dims, ((), ())), precision=precision, preferred_element_type=F32)


def split(a):
    high = a.astype(BF16)
    return high, (a - high.astype(F32)).astype(BF16)


def to_column(row, count):
    rows = lax.broadcasted_iota(jnp.int32, (count, count), 0)
    cols = lax.broadcasted_iota(jnp.int32, (count, count), 1)
    return jnp.sum(jnp.where(rows == cols, row, 0.0), axis=1, keepdims=True)


def to_row(column, count):
    rows = lax.broadcasted_iota(jnp.int32, (count, PAD), 0)
    cols = lax.broadcasted_iota(jnp.int32, (count, PAD), 1)
    return jnp.sum(jnp.where(rows == cols, column, 0.0), axis=0, keepdims=True)


def head_spread(start, size, width):
    rows = lax.broadcasted_iota(jnp.int32, (PAD, size), 0)
    cols = lax.broadcasted_iota(jnp.int32, (PAD, size), 1) + start
    return jnp.where((cols >= rows * width) & (cols < (rows + 1) * width), 1.0, 0.0).astype(F32)


def pad_rows(a):
    return jnp.concatenate([a, jnp.zeros((PAD - a.shape[0], a.shape[1]), a.dtype)], axis=0)


def pair_parts(k, heads, width, x, dy, l_row, l_col):
    tokens = x.shape[0]
    half = tokens // 2
    pair = 2 * width
    rows = lax.broadcasted_iota(jnp.int32, (half, half), 0)
    cols = lax.broadcasted_iota(jnp.int32, (half, half), 1)
    causal = cols >= rows
    in_first = lax.broadcasted_iota(jnp.int32, (1, pair), 1) < width
    keep = [jnp.where(in_first, 1.0, 0.0).astype(BF16), jnp.where(in_first, 0.0, 1.0).astype(BF16)]
    at = pl.ds(pl.multiple_of(k * pair, pair), pair)
    x2 = x[:, at]
    dy2 = dy[:, at]
    columns = pltpu.roll(l_col[...], lax.rem(PAD - 2 * k, PAD), 1)
    sides = []
    for side in range(2):
        l_j = columns[:, side : side + 1]
        l_i = l_row[pl.ds(2 * k + side, 1), :]
        xs = x2 * keep[side]
        w_top = dot(xs[:half], dy2, ((1,), (1,)))
        w_low = dot(xs[half:], dy2[half:], ((1,), (1,)))
        d00 = jnp.exp2(jnp.where(causal, l_i[:, :half] - l_j[:half], -1e30))
        d01 = jnp.exp2(l_i[:, half:] - l_j[:half])
        d11 = jnp.exp2(jnp.where(causal, l_i[:, half:] - l_j[half:], -1e30))
        sides.append(((d00, w_top[:, :half]), (d01, w_top[:, half:]), (d11, w_low)))
    return at, dy2, in_first, sides


def heads_part(heads, width, x, dy, l_row, l_col, qt):
    half = x.shape[0] // 2
    qt[...] = jnp.zeros_like(qt)

    @pl.loop(0, heads // 2)
    def _(k):
        _, _, _, sides = pair_parts(k, heads, width, x, dy, l_row, l_col)
        for n, (j, i) in enumerate(((0, 0), (0, 1), (1, 1))):
            js, at_i = slice(j * half, (j + 1) * half), slice(i * half, (i + 1) * half)
            (d_a, w_a), (d_b, w_b) = sides[0][n], sides[1][n]
            qt[js, at_i] += d_a * w_a + d_b * w_b


def one_pair(k, heads, width, x, dy, l_row, l_col, g, dx, r_row, t_col):
    tokens = x.shape[0]
    half = tokens // 2
    lanes = lax.broadcasted_iota(jnp.int32, (tokens, PAD), 1)
    at, dy2, in_first, sides = pair_parts(k, heads, width, x, dy, l_row, l_col)
    sums = t_col[...]
    pieces = []
    for side in range(2):
        head = 2 * k + side
        (d00, w00), (d01, w01), (d11, w11) = sides[side]
        m00, m01, m11 = d00 * g[:half, :half], d01 * g[:half, half:], d11 * g[half:, half:]
        e00, e01, e11 = m00 * w00, m01 * w01, m11 * w11
        r_row[pl.ds(head, 1), :] = jnp.concatenate(
            [jnp.sum(e00, axis=0, keepdims=True), jnp.sum(e01 + e11, axis=0, keepdims=True)], axis=1
        )
        column = jnp.concatenate(
            [jnp.sum(e00 + e01, axis=1, keepdims=True), jnp.sum(e11, axis=1, keepdims=True)], axis=0
        )
        sums = jnp.where(lanes == head, column, sums)
        top_high, top_low = split(jnp.concatenate([m00, m01], axis=1))
        low_high, low_low = split(m11)
        top = dot(top_high, dy2) + dot(top_low, dy2)
        low = dot(low_high, dy2[half:]) + dot(low_low, dy2[half:])
        pieces.append((top, low))
    t_col[...] = sums
    dx[:half, at] = jnp.where(in_first, pieces[0][0], pieces[1][0])
    dx[half:, at] = jnp.where(in_first, pieces[0][1], pieces[1][1])


def plan(rows, bits, order):
    steps = []
    for bit in order:
        halves = rows % 16 == 0
        rows = rows // 2 if halves else rows
        steps.append((bit, rows, halves))
    return steps


def layer_kernel(
    bits, scenes, plans, chunk_rows, heads, width,
    tile, step, log_rate, gain, hidden_hbm, weight_hbm, x_hbm, dy_hbm,
    grad_x, grad_step, out, rate_out, skip_out,
    hidden, weight, x, dy, zs, tt, rt, back_all, dx, qt, g, l_row, l_col, r_row, t_col, w, small, acc, sacc, *rest
):
    bufs = rest[: len(plans)]
    sbuf, sems_send, sems_recv, sems_load = rest[len(plans) :]
    seq, dp = lax.axis_index("seq"), lax.axis_index("dp")
    first = seq == 0
    share = out.shape[0]
    tokens = x.shape[0]
    state = weight.shape[1] // 2
    slabs = x.shape[1] // SLAB

    def flipped(bit):
        mine = lax.rem(dp // (1 << bit), 2)
        return mine, dp + (1 - 2 * mine) * (1 << bit)

    other = 1 - seq
    loads = [
        pltpu.make_async_copy(src, dst, sems_load.at[n])
        for n, (src, dst) in enumerate(((hidden_hbm, hidden), (weight_hbm, weight), (x_hbm, x), (dy_hbm, dy)))
    ]
    for load in loads:
        load.start()
    barrier = pltpu.get_barrier_semaphore()
    pl.semaphore_signal(barrier, inc=1, device_id=(other, dp), device_id_type=MESH)
    for bit in range(bits):
        pl.semaphore_signal(barrier, inc=1, device_id=(seq, flipped(bit)[1]), device_id_type=MESH)

    count = [0]
    pending = []

    def send(src, dst, target):
        n = count[0]
        count[0] += 1
        copy = pltpu.make_async_remote_copy(
            src_ref=src, dst_ref=dst, send_sem=sems_send.at[n], recv_sem=sems_recv.at[n],
            device_id=target, device_id_type=MESH,
        )
        copy.start()
        pending.append(copy)
        return copy

    mask = jnp.where(tile[0, 0] == 0, 1.0, 0.0).astype(F32)
    on_first = jnp.where(first, 1.0, 0.0).astype(F32)
    rate = -jnp.exp(to_column(log_rate[...], heads))
    masked = step[...] * mask
    rows = lax.broadcasted_iota(jnp.int32, (tokens, tokens), 0)
    cols = lax.broadcasted_iota(jnp.int32, (tokens, tokens), 1)
    running = dot(masked * rate, jnp.where(rows <= cols, 1.0, 0.0).astype(F32), precision=EXACT)
    alpha = jnp.where(first, jnp.exp(running[:, tokens - 1 :] - running) * masked, jnp.exp(running) * mask)
    alpha_high, alpha_low = split(pad_rows(alpha).T)
    both_alpha = jnp.concatenate([alpha_high, alpha_low], axis=1)
    l_row[...] = running * LOG2E
    l_col[...] = pad_rows((running - jnp.log(step[...])) * LOG2E + (1.0 - mask) * 1e30).T

    loads[0].wait()
    loads[1].wait()
    projected = dot(hidden[...], weight[...])
    keys, query = projected[:, :state], projected[:, state:]
    both_keys = jnp.concatenate(split(jnp.where(first, keys, query)), axis=1)
    turned_keys = both_keys.T
    loads[2].wait()
    loads[3].wait()
    pl.semaphore_wait(barrier, bits + 1)
    swaps = []
    for n in range(slabs):
        at = slice(n * SLAB, (n + 1) * SLAB)
        spread = head_spread(n * SLAB, SLAB, width).astype(BF16)
        wide = dot(both_alpha, jnp.concatenate([spread, spread], axis=0))
        z = jnp.where(first, x[:, at].astype(F32), dy[:, at].astype(F32))
        scaled, scaled_low = split(z * wide)
        zs[:, at] = scaled
        both = dot(turned_keys, scaled) + dot(turned_keys, scaled_low)
        tt[n] = both[:state] + both[state:]
        swaps.append(send(tt.at[n], rt.at[n], (other, dp)))

    heads_part(heads, width, x, dy, l_row, l_col, qt)
    key_parts = jnp.concatenate(split(keys), axis=1)
    query_parts = jnp.concatenate(split(query), axis=1)
    q_high, q_low = split(qt[...])
    grad_b = dot(q_high, query_parts) + dot(q_low, query_parts)
    grad_c = dot(q_high, key_parts, ((0,), (0,))) + dot(q_low, key_parts, ((0,), (0,)))
    grad_keys = jnp.zeros((tokens, 2 * state), F32)
    for n in range(slabs):
        swaps[n].wait_recv()
        at = slice(n * SLAB, (n + 1) * SLAB)
        grad_keys += dot(zs[:, at], jnp.concatenate(split(rt[n]), axis=0), ((1,), (1,)))
    grad_b += on_first * grad_keys
    grad_c += (1.0 - on_first) * grad_keys
    grad_p = jnp.concatenate(
        [grad_b[:, :state] + grad_b[:, state:], grad_c[:, :state] + grad_c[:, state:]], axis=1
    ).astype(BF16)

    def aligned(v):
        return pl.multiple_of(v, 8)

    def weight_rows(start, rows):
        w[pl.ds(aligned(start), rows), :] = dot(
            hidden[:, pl.ds(pl.multiple_of(start, PAD), rows)], grad_p, ((0,), (0,))
        )

    chunks = range(len(plans))
    bases = [sum(chunk_rows[:c]) for c in range(len(plans))]
    copies = [None] * len(plans)
    for c in chunks:
        size = chunk_rows[c]
        weight_rows(other * share + bases[c], size)
        copies[c] = send(
            w.at[pl.ds(aligned(other * share + bases[c]), size)], bufs[c].at[pl.ds(0, size)], (other, dp)
        )

    pair_args = (heads, width, x, dy, l_row, l_col, g, dx, r_row, t_col)
    scale = 1.0 / scenes
    terms = {"carried": jnp.zeros((tokens, PAD), F32), "skip": jnp.zeros((8, PAD), F32)}
    light = [-1, None]

    def run_pairs(lo, hi):
        if lo == 0:
            g[...] = dot(keys, query, ((1,), (1,)), EXACT)
            t_col[...] = jnp.zeros_like(t_col)

        @pl.loop(lo, hi)
        def _(k):
            one_pair(k, *pair_args)

    def run_carried(n):
        at = slice(n * SLAB, (n + 1) * SLAB)
        spread = head_spread(n * SLAB, SLAB, width)
        spread_b = spread.astype(BF16)
        r_high, r_low = split(rt[n])
        back = dot(both_keys, jnp.concatenate([r_high, r_high], axis=0)) + dot(both_keys[:, :state], r_low)
        back_all[:, at] = back
        p_high, p_low = split(zs[:, at].astype(F32) * back)
        terms["carried"] += dot(p_high, spread_b, ((1,), (1,))) + dot(p_low, spread_b, ((1,), (1,)))
        total = jnp.sum(x[:, at].astype(F32) * dy[:, at].astype(F32), axis=0, keepdims=True)
        terms["skip"] += dot(jnp.broadcast_to(total, (8, SLAB)), spread, ((1,), (1,)), EXACT)

    def run_input(n):
        at = slice(n * SLAB, (n + 1) * SLAB)
        spread = head_spread(n * SLAB, SLAB, width)
        spread_b = spread.astype(BF16)
        gains = jnp.concatenate([gain[...] * mask, jnp.zeros((1, PAD - heads), F32)], axis=1)
        gain_row = dot(jnp.broadcast_to(gains, (8, PAD)), spread, precision=EXACT)[0:1]
        wide = dot(both_alpha, jnp.concatenate([spread_b, spread_b], axis=0)) * on_first
        grad_x[:, at] = (dx[:, at] + wide * back_all[:, at] + gain_row * dy[:, at].astype(F32)).astype(BF16)

    def run_last():
        crossing = terms["carried"].T[:heads]
        weighted = t_col[...].T[:heads]
        sign = 1.0 - 2.0 * on_first
        grad_l = r_row[...] - weighted + sign * crossing
        upper = jnp.where(rows >= cols, 1.0, 0.0).astype(F32)
        grad_log = dot(grad_l, upper, precision=EXACT)
        grad_log += on_first * jnp.sum(crossing, axis=1, keepdims=True)
        grad_step[...] = mask * ((weighted + on_first * crossing) / step[...] + rate * grad_log)
        grad_rate = jnp.sum(grad_log * masked, axis=1, keepdims=True) * rate
        row = lax.broadcasted_iota(jnp.int32, (8, PAD), 0)
        small[...] = jnp.where(row == 0, to_row(grad_rate, heads), jnp.where(row == 1, terms["skip"] * mask, 0.0))
        advance_small()

    def advance_small():
        stage = light[0]
        if stage > bits:
            return
        if stage >= 0:
            light[1].wait_recv()
            sacc[stage] = (small[...] if stage == 0 else sacc[stage - 1]) + sbuf[stage]
        light[0] = stage = stage + 1
        if stage == 0:
            light[1] = send(small, sbuf.at[0], (other, dp))
        elif stage <= bits:
            light[1] = send(sacc.at[stage - 1], sbuf.at[stage], (seq, flipped(stage - 1)[1]))

    quotas = list(QUOTAS)
    done = [0]
    pairs = heads // 2
    work = [functools.partial(run_carried, n) for n in range(slabs)] + [run_last]
    work += [functools.partial(run_input, n) for n in range(slabs)]

    def tick():
        n = quotas.pop(0) if quotas else 1
        if light[0] >= 0:
            advance_small()
        end = min(done[0] + n, pairs + len(work))
        if done[0] < min(end, pairs):
            run_pairs(done[0], min(end, pairs))
        for unit in range(max(done[0], pairs), end):
            work[unit - pairs]()
        done[0] = max(end, done[0])

    starts = list(bases)
    offsets = list(chunk_rows)
    history = [[] for _ in plans]

    def start_step(c, s):
        bit, kept, halves = plans[c][s]
        side, peer = flipped(bit)
        begin = starts[c]
        source = begin
        if halves:
            source = aligned(begin + (1 - side) * kept)
            starts[c] = aligned(begin + side * kept)
        offset = offsets[c]
        offsets[c] = offset + kept
        history[c].append((bit, kept, halves, starts[c]))
        copies[c] = send(acc.at[pl.ds(source, kept)], bufs[c].at[pl.ds(offset, kept)], (seq, peer))

    for c in chunks:
        weight_rows(seq * share + bases[c], chunk_rows[c])
    tick()
    for c in chunks:
        rows_here = chunk_rows[c]
        copies[c].wait_recv()
        mine = w[pl.ds(aligned(seq * share + bases[c]), rows_here), :]
        acc[pl.ds(bases[c], rows_here), :] = mine + bufs[c][0:rows_here, :]
        start_step(c, 0)

    for s in range(bits):
        for c in chunks:
            tick()
            kept, halves = plans[c][s][1:]
            copies[c].wait_recv()
            if not halves:
                copies[c].wait_send()
                pending[:] = [p for p in pending if p is not copies[c]]
            here = pl.ds(starts[c], kept)
            acc[here, :] = acc[here, :] + bufs[c][offsets[c] - kept : offsets[c], :]
            if s + 1 < bits:
                start_step(c, s + 1)
            else:
                out[here, :] = acc[here, :] * scale

    trail = [[h for h in reversed(history[c]) if h[2]] for c in range(len(plans))]

    def gather(c, n):
        bit, kept, _, start = trail[c][n]
        region = out.at[pl.ds(start, kept)]
        return send(region, region, (seq, flipped(bit)[1]))

    for c in chunks:
        copies[c] = gather(c, 0)
    for n in range(max(len(t) for t in trail)):
        for c in chunks:
            if n < len(trail[c]):
                tick()
                copies[c].wait_recv()
                if n + 1 < len(trail[c]):
                    copies[c] = gather(c, n + 1)
    while light[0] <= bits or done[0] < pairs + len(work):
        tick()
    total = sacc[bits] * scale
    total = jnp.where(seq == 0, total, pltpu.roll(total, PAD - heads // 2, 1))
    rate_out[...] = total[0:1, : heads // 2]
    skip_out[...] = total[1:2, : heads // 2]
    for copy in pending:
        copy.wait_send()


def emit_kernel(*refs):
    count = len(refs) // 2
    copies = [pltpu.make_async_copy(refs[n], refs[count + n], refs[-1].at[n]) for n in range(count)]
    for copy in copies:
        copy.start()
    for copy in copies:
        copy.wait()


def chunk_orders(bits):
    if bits < 4:
        return [list(range(bits))] * 3
    late = list(range(3, bits))
    return [0, 2, 1] + late, [1, 0, 2] + late, [2, 1, 0] + late


def shards(hidden, scan_input, grad_out, step_size, proj_weight, log_rate, skip_gain, tile_list):
    tokens, inner = scan_input.shape[1:]
    model, two_state = proj_weight.shape
    heads = log_rate.shape[0]
    width = inner // heads
    slabs, state = inner // SLAB, two_state // 2
    scenes, seqs = lax.axis_size("dp"), lax.axis_size("seq")
    bits = scenes.bit_length() - 1
    rows = model // seqs
    low = rows // (3 * PAD) * PAD
    chunk_rows = (low, low, rows - 2 * low)
    plans = [plan(r, bits, o) for r, o in zip(chunk_rows, chunk_orders(bits))]

    def shape(*dims, dtype=F32):
        return jax.ShapeDtypeStruct(dims, dtype)

    scratch = [
        pltpu.VMEM((tokens, model), BF16), pltpu.VMEM((model, two_state), BF16),
        pltpu.VMEM((tokens, inner), BF16), pltpu.VMEM((tokens, inner), BF16), pltpu.VMEM((tokens, inner), BF16),
        pltpu.VMEM((slabs, state, SLAB), F32), pltpu.VMEM((slabs, state, SLAB), F32),
        pltpu.VMEM((tokens, inner), F32), pltpu.VMEM((tokens, inner), F32),
        pltpu.VMEM((tokens, tokens), F32), pltpu.VMEM((tokens, tokens), F32),
        pltpu.VMEM((heads, tokens), F32), pltpu.VMEM((tokens, PAD), F32),
        pltpu.VMEM((heads, tokens), F32), pltpu.VMEM((tokens, PAD), F32),
        pltpu.VMEM((model, two_state), F32), pltpu.VMEM((8, PAD), F32),
        pltpu.VMEM((rows, two_state), F32), pltpu.VMEM((bits + 1, 8, PAD), F32),
    ]
    for r, steps in zip(chunk_rows, plans):
        scratch.append(pltpu.VMEM((r + sum(k for _, k, _ in steps), two_state), F32))
    scratch.append(pltpu.VMEM((bits + 1, 8, PAD), F32))
    copies = slabs + len(plans) * (1 + 2 * bits) + bits + 1
    scratch += [pltpu.SemaphoreType.DMA((copies,)), pltpu.SemaphoreType.DMA((copies,)), pltpu.SemaphoreType.DMA((4,))]
    anywhere = pl.BlockSpec(memory_space=pl.ANY)
    out_shape = (
        shape(tokens, inner, dtype=BF16), shape(heads, tokens), shape(rows, two_state),
        shape(1, heads // seqs), shape(1, heads // seqs),
    )
    outs = pl.pallas_call(
        functools.partial(layer_kernel, bits, scenes, plans, chunk_rows, heads, width),
        out_shape=out_shape,
        in_specs=[SMEM] + [VMEM] * 3 + [anywhere] * 4,
        out_specs=(VMEM,) * 5,
        scratch_shapes=scratch,
        compiler_params=pltpu.CompilerParams(
            collective_id=0, has_side_effects=True, vmem_limit_bytes=48 * 1024 * 1024
        ),
        name="layer",
    )(
        tile_list, step_size[0], log_rate[None], skip_gain[None],
        hidden[0], proj_weight, scan_input[0], grad_out[0],
    )
    grad_x, grad_step, summed, rates, gains = pl.pallas_call(
        emit_kernel,
        out_shape=out_shape,
        in_specs=[anywhere] * 5,
        out_specs=(anywhere,) * 5,
        scratch_shapes=[pltpu.SemaphoreType.DMA((5,))],
        name="emit",
    )(*outs)
    return grad_x[None], grad_step[None], summed, rates[0], gains[0]


def solution(mesh):
    in_specs = (
        P("dp", "seq", None),
        P("dp", "seq", None),
        P("dp", "seq", None),
        P("dp", None, "seq"),
        P(),
        P(),
        P(),
        P("dp", "seq"),
    )
    out_specs = (P("dp", "seq", None), P("dp", None, "seq"), P("seq", None), P("seq"), P("seq"))
    return jax.shard_map(shards, mesh=mesh, in_specs=in_specs, out_specs=out_specs, check_vma=False)
```

time: 72.4 us -> 150 us (2.07)
  Pallas kernels: 65.6 us -> 140 us
  local copies, waits for them, and re-layouts: 4.73 us -> 8.56 us
    pallas_call x3 -> x2, Pallas kernels: 65.6 us -> 140 us  [the longest x1 81.8 us: shards(): pl.pallas_call(emit_kernel, out_shape=out_shape, in_specs=[anywhere] * 5,...]
    unnamed x23 -> x20, local copies, waits for them, and re-layouts: 4.73 us -> 8.56 us
  transfers between devices with their start and end apart: 1 -> 0, of which waited for: 0 -> 0; matrix products, arithmetic and copies ran while one was open for 0% -> 0% of each run, Pallas kernels for 11% -> 0%
where the time goes in v2:
time: 150 us
  Pallas kernels  140 us (93%)
  local copies, waits for them, and re-layouts  8.56 us (6%)
    pallas_call x1, Pallas kernels, shards(): pl.pallas_call(emit_kernel, out_shape=out_shape, in_specs=[anywhere] * 5,...  81.8 us
    pallas_call x1, Pallas kernels, shards(): pl.pallas_call(functools.partial(layer_kernel, bits, scenes, plans, chunk...  58.1 us
    unnamed x20, local copies, waits for them, and re-layouts  8.56 us

profile of v2, /device:TPU:0, one launch (start us, length us, event | category | flops | bytes accessed | tf_op | source)
XLA Modules:
  0.0 149.9 jit_solution(3403334728843035792)
XLA Ops:
  1.3 0.0 copy-start.2
  1.3 1.3 copy-done.2
  2.6 0.0 copy-start.3
  2.6 1.3 copy-done.3
  3.9 0.0 copy-start.4
  3.9 0.8 copy-done.4
  4.7 0.0 copy-start.6
  4.7 0.7 copy-done.6
  5.3 0.0 copy-start.7
  5.4 0.7 copy-done.7
  6.0 58.1 %layer.1 = (bf16[256,2560]{1,0:T(8,128)(2,1)S(1)}, f32[40,256]{1,0:T(8,128)S(1)}, f32[1280,256]{1,0:T(8,128)S(1)}, f32[1,20]{1,0:T(1,128)S(1)}, f32[1,20]{1,0:T(1,128)S(1)}) custom-call(s32[1,1]{1,0:T(1,128)S(6)} %copy.13.tile, f32[40,256]{1,0:T(8,128)S(1)} %bitcast.11, f32[1,40]{1,0:T(1,128)S(1)} %bitcast.12, f32[1,40]{1,0:T(1,128)S(1)} %bitcast.13, ...), custom_call_target="tpu_custom_call" | custom-call | tf_op jit(solution)/shard_map/layer/pallas_call | solution.py:445
  64.1 0.0 copy-start
  64.1 1.1 copy-done
  65.2 0.0 copy-start.1
  65.2 1.1 copy-done.1
  66.3 0.0 copy-start.5
  66.3 0.6 copy-done.5
  66.9 0.0 copy-start.8
  66.9 0.5 copy-done.8
  67.4 0.0 copy-start.9
  67.4 0.6 copy-done.9
  68.0 81.8 %emit.1 = (bf16[256,2560]{1,0:T(8,128)(2,1)}, f32[40,256]{1,0:T(8,128)}, f32[1280,256]{1,0:T(8,128)}, f32[1,20]{1,0:T(1,128)}, f32[1,20]{1,0:T(1,128)}) custom-call(bf16[256,2560]{1,0:T(8,128)(2,1)} %copy-done, f32[40,256]{1,0:T(8,128)} %copy-done.5, f32[1280,256]{1,0:T(8,128)} %copy-done.1, f32[1,20]{1,0:T(1,128)} %copy-done.8, f32[1,20]{1,0:T(1,128)} %copy-done.9), custom_call_target="tpu_custom_call" | custom-call | tf_op jit(solution)/shard_map/emit/pallas_call | solution.py:459
Async XLA Ops:
  1.3 1.3 copy-start.2
  2.6 1.3 copy-start.3
  3.9 0.8 copy-start.4
  4.7 0.7 copy-start.6
  5.3 0.7 copy-start.7
  64.1 1.1 copy-start
  65.2 1.1 copy-start.1
  66.3 0.6 copy-start.5
  66.9 0.5 copy-start.8
  67.4 0.6 copy-start.9

commit v3 on v2

--- a/solution.py
+++ b/solution.py
@@ -14,7 +14,7 @@
 LOG2E = 1.4426950408889634
 PAD = 128
 SLAB = 512
-QUOTAS = (1, 5, 1, 0, 2, 1, 0, 1, 1, 0, 3, 1, 0, 2, 1, 1, 3, 2, 1, 0, 1, 1, 1, 1, 1)
+QUOTAS = (2, 6, 0, 0, 4, 0, 0, 2, 2, 0, 4, 1, 0, 2, 1, 0, 1, 1, 0, 1, 1, 0, 1, 1, 1)
 VMEM = pl.BlockSpec(memory_space=pltpu.VMEM)
 SMEM = pl.BlockSpec(memory_space=pltpu.SMEM)
 
@@ -50,7 +50,7 @@
     return jnp.concatenate([a, jnp.zeros((PAD - a.shape[0], a.shape[1]), a.dtype)], axis=0)
 
 
-def pair_parts(k, heads, width, x, dy, l_row, l_col):
+def pair_parts(k, turned, lane, width, x, dy, l_row):
     tokens = x.shape[0]
     half = tokens // 2
     pair = 2 * width
@@ -62,10 +62,9 @@
     at = pl.ds(pl.multiple_of(k * pair, pair), pair)
     x2 = x[:, at]
     dy2 = dy[:, at]
-    columns = pltpu.roll(l_col[...], lax.rem(PAD - 2 * k, PAD), 1)
     sides = []
     for side in range(2):
-        l_j = columns[:, side : side + 1]
+        l_j = turned[:, lane + side : lane + side + 1]
         l_i = l_row[pl.ds(2 * k + side, 1), :]
         xs = x2 * keep[side]
         w_top = dot(xs[:half], dy2, ((1,), (1,)))
@@ -77,24 +76,31 @@
     return at, dy2, in_first, sides
 
 
+def turn(l_col, k):
+    return pltpu.roll(l_col[...], lax.rem(PAD - 2 * k, PAD), 1)
+
+
 def heads_part(heads, width, x, dy, l_row, l_col, qt):
     half = x.shape[0] // 2
     qt[...] = jnp.zeros_like(qt)
-
-    @pl.loop(0, heads // 2)
-    def _(k):
-        _, _, _, sides = pair_parts(k, heads, width, x, dy, l_row, l_col)
+    group = 4 if heads % 8 == 0 else 1
+
+    @pl.loop(0, heads // 2 // group)
+    def _(step):
+        turned = turn(l_col, step * group)
+        parts = []
+        for n in range(group):
+            parts += pair_parts(step * group + n, turned, 2 * n, width, x, dy, l_row)[3]
         for n, (j, i) in enumerate(((0, 0), (0, 1), (1, 1))):
             js, at_i = slice(j * half, (j + 1) * half), slice(i * half, (i + 1) * half)
-            (d_a, w_a), (d_b, w_b) = sides[0][n], sides[1][n]
-            qt[js, at_i] += d_a * w_a + d_b * w_b
-
-
-def one_pair(k, heads, width, x, dy, l_row, l_col, g, dx, r_row, t_col):
+            qt[js, at_i] += sum(side[n][0] * side[n][1] for side in parts)
+
+
+def one_pair(k, turned, lane, width, x, dy, l_row, g, dx, r_row, t_col):
     tokens = x.shape[0]
     half = tokens // 2
     lanes = lax.broadcasted_iota(jnp.int32, (tokens, PAD), 1)
-    at, dy2, in_first, sides = pair_parts(k, heads, width, x, dy, l_row, l_col)
+    at, dy2, in_first, sides = pair_parts(k, turned, lane, width, x, dy, l_row)
     sums = t_col[...]
     pieces = []
     for side in range(2):
@@ -130,9 +136,9 @@
 
 def layer_kernel(
     bits, scenes, plans, chunk_rows, heads, width,
-    tile, step, log_rate, gain, hidden_hbm, weight_hbm, x_hbm, dy_hbm,
+    tile, step_hbm, rate_hbm, gain_hbm, hidden_hbm, weight_hbm, x_hbm, dy_hbm,
     grad_x, grad_step, out, rate_out, skip_out,
-    hidden, weight, x, dy, zs, tt, rt, back_all, dx, qt, g, l_row, l_col, r_row, t_col, w, small, acc, sacc, *rest
+    step, log_rate, gain, hidden, weight, x, dy, spread_all, zs, tt, rt, back_all, dx, qt, g, l_row, l_col, r_row, t_col, w, small, acc, sacc, *rest
 ):
     bufs = rest[: len(plans)]
     sbuf, sems_send, sems_recv, sems_load = rest[len(plans) :]
@@ -150,7 +156,10 @@
     other = 1 - seq
     loads = [
         pltpu.make_async_copy(src, dst, sems_load.at[n])
-        for n, (src, dst) in enumerate(((hidden_hbm, hidden), (weight_hbm, weight), (x_hbm, x), (dy_hbm, dy)))
+        for n, (src, dst) in enumerate((
+            (step_hbm, step), (rate_hbm, log_rate), (gain_hbm, gain),
+            (hidden_hbm, hidden), (weight_hbm, weight), (x_hbm, x), (dy_hbm, dy),
+        ))
     ]
     for load in loads:
         load.start()
@@ -173,6 +182,10 @@
         pending.append(copy)
         return copy
 
+    for n in range(slabs):
+        spread_all[:, n * SLAB : (n + 1) * SLAB] = head_spread(n * SLAB, SLAB, width).astype(BF16)
+    for load in loads[:3]:
+        load.wait()
     mask = jnp.where(tile[0, 0] == 0, 1.0, 0.0).astype(F32)
     on_first = jnp.where(first, 1.0, 0.0).astype(F32)
     rate = -jnp.exp(to_column(log_rate[...], heads))
@@ -183,22 +196,24 @@
     alpha = jnp.where(first, jnp.exp(running[:, tokens - 1 :] - running) * masked, jnp.exp(running) * mask)
     alpha_high, alpha_low = split(pad_rows(alpha).T)
     both_alpha = jnp.concatenate([alpha_high, alpha_low], axis=1)
+    gains = jnp.concatenate([gain[...] * mask, jnp.zeros((1, PAD - heads), F32)], axis=1)
+    gain_parts = jnp.concatenate(split(jnp.broadcast_to(gains, (16, PAD))), axis=1)
     l_row[...] = running * LOG2E
     l_col[...] = pad_rows((running - jnp.log(step[...])) * LOG2E + (1.0 - mask) * 1e30).T
 
-    loads[0].wait()
-    loads[1].wait()
+    loads[3].wait()
+    loads[4].wait()
     projected = dot(hidden[...], weight[...])
     keys, query = projected[:, :state], projected[:, state:]
     both_keys = jnp.concatenate(split(jnp.where(first, keys, query)), axis=1)
     turned_keys = both_keys.T
-    loads[2].wait()
-    loads[3].wait()
+    loads[5].wait()
+    loads[6].wait()
     pl.semaphore_wait(barrier, bits + 1)
     swaps = []
     for n in range(slabs):
         at = slice(n * SLAB, (n + 1) * SLAB)
-        spread = head_spread(n * SLAB, SLAB, width).astype(BF16)
+        spread = spread_all[:, at]
         wide = dot(both_alpha, jnp.concatenate([spread, spread], axis=0))
         z = jnp.where(first, x[:, at].astype(F32), dy[:, at].astype(F32))
         scaled, scaled_low = split(z * wide)
@@ -242,7 +257,7 @@
             w.at[pl.ds(aligned(other * share + bases[c]), size)], bufs[c].at[pl.ds(0, size)], (other, dp)
         )
 
-    pair_args = (heads, width, x, dy, l_row, l_col, g, dx, r_row, t_col)
+    pair_args = (width, x, dy, l_row, g, dx, r_row, t_col)
     scale = 1.0 / scenes
     terms = {"carried": jnp.zeros((tokens, PAD), F32), "skip": jnp.zeros((8, PAD), F32)}
     light = [-1, None]
@@ -252,29 +267,37 @@
             g[...] = dot(keys, query, ((1,), (1,)), EXACT)
             t_col[...] = jnp.zeros_like(t_col)
 
-        @pl.loop(lo, hi)
-        def _(k):
-            one_pair(k, *pair_args)
+        if hi - lo > 1:
+
+            @pl.loop(0, (hi - lo) // 2)
+            def _(n):
+                turned = turn(l_col, lo + 2 * n)
+                one_pair(lo + 2 * n, turned, 0, *pair_args)
+                one_pair(lo + 2 * n + 1, turned, 2, *pair_args)
+
+        if (hi - lo) % 2:
+            one_pair(hi - 1, turn(l_col, hi - 1), 0, *pair_args)
 
     def run_carried(n):
         at = slice(n * SLAB, (n + 1) * SLAB)
-        spread = head_spread(n * SLAB, SLAB, width)
-        spread_b = spread.astype(BF16)
+        spread = spread_all[:, at]
         r_high, r_low = split(rt[n])
         back = dot(both_keys, jnp.concatenate([r_high, r_high], axis=0)) + dot(both_keys[:, :state], r_low)
         back_all[:, at] = back
         p_high, p_low = split(zs[:, at].astype(F32) * back)
-        terms["carried"] += dot(p_high, spread_b, ((1,), (1,))) + dot(p_low, spread_b, ((1,), (1,)))
         total = jnp.sum(x[:, at].astype(F32) * dy[:, at].astype(F32), axis=0, keepdims=True)
-        terms["skip"] += dot(jnp.broadcast_to(total, (8, SLAB)), spread, ((1,), (1,)), EXACT)
+        t_high, t_low = split(jnp.broadcast_to(total, (16, SLAB)))
+        summed = dot(jnp.concatenate([p_high, p_low, t_high, t_low], axis=0), spread, ((1,), (1,)))
+        terms["carried"] += summed[:tokens] + summed[tokens : 2 * tokens]
+        terms["skip"] += summed[2 * tokens : 2 * tokens + 8] + summed[2 * tokens + 16 : 2 * tokens + 24]
 
     def run_input(n):
         at = slice(n * SLAB, (n + 1) * SLAB)
-        spread = head_spread(n * SLAB, SLAB, width)
-        spread_b = spread.astype(BF16)
-        gains = jnp.concatenate([gain[...] * mask, jnp.zeros((1, PAD - heads), F32)], axis=1)
-        gain_row = dot(jnp.broadcast_to(gains, (8, PAD)), spread, precision=EXACT)[0:1]
-        wide = dot(both_alpha, jnp.concatenate([spread_b, spread_b], axis=0)) * on_first
+        spread = spread_all[:, at]
+        both = dot(
+            jnp.concatenate([both_alpha, gain_parts], axis=0), jnp.concatenate([spread, spread], axis=0)
+        )
+        wide, gain_row = both[:tokens] * on_first, both[tokens : tokens + 1]
         grad_x[:, at] = (dx[:, at] + wide * back_all[:, at] + gain_row * dy[:, at].astype(F32)).astype(BF16)
 
     def run_last():
@@ -391,11 +414,8 @@
 
 def emit_kernel(*refs):
     count = len(refs) // 2
-    copies = [pltpu.make_async_copy(refs[n], refs[count + n], refs[-1].at[n]) for n in range(count)]
-    for copy in copies:
-        copy.start()
-    for copy in copies:
-        copy.wait()
+    for n in range(count):
+        refs[count + n][...] = refs[n][...]
 
 
 def chunk_orders(bits):
@@ -422,8 +442,10 @@
         return jax.ShapeDtypeStruct(dims, dtype)
 
     scratch = [
+        pltpu.VMEM((heads, tokens), F32), pltpu.VMEM((1, heads), F32), pltpu.VMEM((1, heads), F32),
         pltpu.VMEM((tokens, model), BF16), pltpu.VMEM((model, two_state), BF16),
-        pltpu.VMEM((tokens, inner), BF16), pltpu.VMEM((tokens, inner), BF16), pltpu.VMEM((tokens, inner), BF16),
+        pltpu.VMEM((tokens, inner), BF16), pltpu.VMEM((tokens, inner), BF16),
+        pltpu.VMEM((PAD, inner), BF16), pltpu.VMEM((tokens, inner), BF16),
         pltpu.VMEM((slabs, state, SLAB), F32), pltpu.VMEM((slabs, state, SLAB), F32),
         pltpu.VMEM((tokens, inner), F32), pltpu.VMEM((tokens, inner), F32),
         pltpu.VMEM((tokens, tokens), F32), pltpu.VMEM((tokens, tokens), F32),
@@ -436,8 +458,8 @@
         scratch.append(pltpu.VMEM((r + sum(k for _, k, _ in steps), two_state), F32))
     scratch.append(pltpu.VMEM((bits + 1, 8, PAD), F32))
     copies = slabs + len(plans) * (1 + 2 * bits) + bits + 1
-    scratch += [pltpu.SemaphoreType.DMA((copies,)), pltpu.SemaphoreType.DMA((copies,)), pltpu.SemaphoreType.DMA((4,))]
-    anywhere = pl.BlockSpec(memory_space=pl.ANY)
+    scratch += [pltpu.SemaphoreType.DMA((copies,)), pltpu.SemaphoreType.DMA((copies,)), pltpu.SemaphoreType.DMA((7,))]
+    stored = pl.BlockSpec(memory_space=pltpu.HBM)
     out_shape = (
         shape(tokens, inner, dtype=BF16), shape(heads, tokens), shape(rows, two_state),
         shape(1, heads // seqs), shape(1, heads // seqs),
@@ -445,7 +467,7 @@
     outs = pl.pallas_call(
         functools.partial(layer_kernel, bits, scenes, plans, chunk_rows, heads, width),
         out_shape=out_shape,
-        in_specs=[SMEM] + [VMEM] * 3 + [anywhere] * 4,
+        in_specs=[SMEM] + [stored] * 7,
         out_specs=(VMEM,) * 5,
         scratch_shapes=scratch,
         compiler_params=pltpu.CompilerParams(
@@ -459,9 +481,8 @@
     grad_x, grad_step, summed, rates, gains = pl.pallas_call(
         emit_kernel,
         out_shape=out_shape,
-        in_specs=[anywhere] * 5,
-        out_specs=(anywhere,) * 5,
-        scratch_shapes=[pltpu.SemaphoreType.DMA((5,))],
+        in_specs=[VMEM] * 5,
+        out_specs=(VMEM,) * 5,
         name="emit",
     )(*outs)
     return grad_x[None], grad_step[None], summed, rates[0], gains[0]

time: 150 us -> 72 us (0.48)
  Pallas kernels: 140 us -> 61.8 us
    pallas_call x1, Pallas kernels: 81.8 us -> 3.32 us  [shards(): pl.pallas_call(emit_kernel, out_shape=out_shape, in_specs=[VMEM] * 5, out...]
where the time goes in v3:
time: 72 us; the launch traced here: 71.7 us
  Pallas kernels  61.8 us (86%)
  local copies, waits for them, and re-layouts  8.56 us (12%)
  between operations  1.31 us (2%)
    pallas_call x1, Pallas kernels, shards(): pl.pallas_call(functools.partial(layer_kernel, bits, scenes, plans, chunk...  58.5 us
    unnamed x20, local copies, waits for them, and re-layouts  8.56 us
    pallas_call x1, Pallas kernels, shards(): pl.pallas_call(emit_kernel, out_shape=out_shape, in_specs=[VMEM] * 5, out...  3.32 us

profile of v3, /device:TPU:0, one launch (start us, length us, event | category | flops | bytes accessed | tf_op | source)
XLA Modules:
  0.0 71.7 jit_solution(339021786714363309)
XLA Ops:
  1.3 0.0 copy-start.2
  1.3 1.3 %copy-done.2 = bf16[1,256,2560]{2,1,0:T(8,128)(2,1)S(1)} copy-done((bf16[1,256,2560]{2,1,0:T(8,128)(2,1)S(1)}, bf16[1,256,2560]{2,1,0:T(8,128)(2,1)}, u32[]{:S(2)}) %copy-start.2) | copy-done | bytes 1310744
  2.6 0.0 copy-start.3
  2.6 1.3 %copy-done.3 = bf16[2560,256]{1,0:T(8,128)(2,1)S(1)} copy-done((bf16[2560,256]{1,0:T(8,128)(2,1)S(1)}, bf16[2560,256]{1,0:T(8,128)(2,1)}, u32[]{:S(2)}) %copy-start.3) | copy-done | bytes 1310744
  3.9 0.0 copy-start.4
  3.9 0.8 %copy-done.4 = f32[1,40,256]{2,1,0:T(8,128)S(1)} copy-done((f32[1,40,256]{2,1,0:T(8,128)S(1)}, f32[1,40,256]{2,1,0:T(8,128)}, u32[]{:S(2)}) %copy-start.4) | copy-done | bytes 40984
  4.7 0.0 copy-start.6
  4.7 0.7 copy-done.6
  5.3 0.0 copy-start.7
  5.4 0.7 copy-done.7
  6.0 58.5 %layer.1 = (bf16[256,2560]{1,0:T(8,128)(2,1)S(1)}, f32[40,256]{1,0:T(8,128)S(1)}, f32[1280,256]{1,0:T(8,128)S(1)}, f32[1,20]{1,0:T(1,128)S(1)}, f32[1,20]{1,0:T(1,128)S(1)}) custom-call(s32[1,1]{1,0:T(1,128)S(6)} %copy.13.tile, f32[40,256]{1,0:T(8,128)S(1)} %bitcast.11, f32[1,40]{1,0:T(1,128)S(1)} %bitcast.12, f32[1,40]{1,0:T(1,128)S(1)} %bitcast.13, ...), custom_call_target="tpu_custom_call" | custom-call | tf_op jit(solution)/shard_map/layer/pallas_call | solution.py:467
  64.5 0.0 copy-start
  64.5 1.1 %copy-done = bf16[256,2560]{1,0:T(8,128)(2,1)} copy-done((bf16[256,2560]{1,0:T(8,128)(2,1)}, bf16[256,2560]{1,0:T(8,128)(2,1)S(1)}, u32[]{:S(2)}) %copy-start) | copy-done | bytes 1310744
  65.6 0.0 copy-start.1
  65.6 1.1 %copy-done.1 = f32[1280,256]{1,0:T(8,128)} copy-done((f32[1280,256]{1,0:T(8,128)}, f32[1280,256]{1,0:T(8,128)S(1)}, u32[]{:S(2)}) %copy-start.1) | copy-done | bytes 1310744
  66.7 0.0 copy-start.5
  66.7 0.6 copy-done.5
  67.3 0.0 copy-start.8
  67.3 0.5 copy-done.8
  67.8 0.0 copy-start.9
  67.8 0.6 copy-done.9
  68.4 3.3 %emit.1 = (bf16[256,2560]{1,0:T(8,128)(2,1)}, f32[40,256]{1,0:T(8,128)}, f32[1280,256]{1,0:T(8,128)}, f32[1,20]{1,0:T(1,128)}, f32[1,20]{1,0:T(1,128)}) custom-call(bf16[256,2560]{1,0:T(8,128)(2,1)} %copy-done, f32[40,256]{1,0:T(8,128)} %copy-done.5, f32[1280,256]{1,0:T(8,128)} %copy-done.1, f32[1,20]{1,0:T(1,128)} %copy-done.8, f32[1,20]{1,0:T(1,128)} %copy-done.9), custom_call_target="tpu_custom_call" | custom-call | tf_op jit(solution)/shard_map/emit/pallas_call | solution.py:481
Async XLA Ops:
  1.3 1.3 %copy-start.2 = (bf16[1,256,2560]{2,1,0:T(8,128)(2,1)S(1)}, bf16[1,256,2560]{2,1,0:T(8,128)(2,1)}, u32[]{:S(2)}) copy-start(bf16[1,256,2560]{2,1,0:T(8,128)(2,1)} %param.8) | copy-start | bytes 3932164
  2.6 1.3 %copy-start.3 = (bf16[2560,256]{1,0:T(8,128)(2,1)S(1)}, bf16[2560,256]{1,0:T(8,128)(2,1)}, u32[]{:S(2)}) copy-start(bf16[2560,256]{1,0:T(8,128)(2,1)} %weight_hbm.1) | copy-start | bytes 3932164
  3.9 0.8 %copy-start.4 = (f32[1,40,256]{2,1,0:T(8,128)S(1)}, f32[1,40,256]{2,1,0:T(8,128)}, u32[]{:S(2)}) copy-start(f32[1,40,256]{2,1,0:T(8,128)} %param.11) | copy-start | bytes 122884
  4.7 0.7 copy-start.6
  5.3 0.7 copy-start.7
  64.5 1.1 %copy-start = (bf16[256,2560]{1,0:T(8,128)(2,1)}, bf16[256,2560]{1,0:T(8,128)(2,1)S(1)}, u32[]{:S(2)}) copy-start(bf16[256,2560]{1,0:T(8,128)(2,1)S(1)} %get-tuple-element.15.refs_0_) | copy-start | bytes 3932164
  65.6 1.1 %copy-start.1 = (f32[1280,256]{1,0:T(8,128)}, f32[1280,256]{1,0:T(8,128)S(1)}, u32[]{:S(2)}) copy-start(f32[1280,256]{1,0:T(8,128)S(1)} %get-tuple-element.17.refs_2_) | copy-start | bytes 3932164
  66.7 0.6 copy-start.5
  67.3 0.5 copy-start.8
  67.8 0.6 copy-start.9

commit v4 on v3

--- a/solution.py
+++ b/solution.py
@@ -412,12 +412,6 @@
         copy.wait_send()
 
 
-def emit_kernel(*refs):
-    count = len(refs) // 2
-    for n in range(count):
-        refs[count + n][...] = refs[n][...]
-
-
 def chunk_orders(bits):
     if bits < 4:
         return [list(range(bits))] * 3
@@ -464,27 +458,20 @@
         shape(tokens, inner, dtype=BF16), shape(heads, tokens), shape(rows, two_state),
         shape(1, heads // seqs), shape(1, heads // seqs),
     )
-    outs = pl.pallas_call(
+    grad_x, grad_step, summed, rates, gains = pl.pallas_call(
         functools.partial(layer_kernel, bits, scenes, plans, chunk_rows, heads, width),
         out_shape=out_shape,
         in_specs=[SMEM] + [stored] * 7,
         out_specs=(VMEM,) * 5,
         scratch_shapes=scratch,
         compiler_params=pltpu.CompilerParams(
-            collective_id=0, has_side_effects=True, vmem_limit_bytes=48 * 1024 * 1024
+            collective_id=0, has_side_effects=True, vmem_limit_bytes=60 * 1024 * 1024
         ),
         name="layer",
     )(
         tile_list, step_size[0], log_rate[None], skip_gain[None],
         hidden[0], proj_weight, scan_input[0], grad_out[0],
     )
-    grad_x, grad_step, summed, rates, gains = pl.pallas_call(
-        emit_kernel,
-        out_shape=out_shape,
-        in_specs=[VMEM] * 5,
-        out_specs=(VMEM,) * 5,
-        name="emit",
-    )(*outs)
     return grad_x[None], grad_step[None], summed, rates[0], gains[0]
 
 

time: 72 us -> 66.7 us (0.926)
  local copies, waits for them, and re-layouts: 8.56 us -> 5.27 us
  Pallas kernels: 61.8 us -> 59.9 us
    pallas_call x1 -> x0, Pallas kernels: 3.32 us -> none  [shards(): pl.pallas_call(emit_kernel, out_shape=out_shape, in_specs=[VMEM] * 5, out...]
    unnamed x20 -> x13, local copies, waits for them, and re-layouts: 8.56 us -> 5.27 us
    pallas_call x1, Pallas kernels: 58.5 us -> 59.9 us  [shards(): pl.pallas_call(functools.partial(layer_kernel, bits, scenes, plans, chunk...]
where the time goes in v4:
time: 66.7 us; the launch traced here: 66.5 us
  Pallas kernels  59.9 us (90%)
  local copies, waits for them, and re-layouts  5.27 us (8%)
  between operations  1.31 us (2%)
    pallas_call x1, Pallas kernels, shards(): pl.pallas_call(functools.partial(layer_kernel, bits, scenes, plans, chunk...  59.9 us
    unnamed x13, local copies, waits for them, and re-layouts  5.27 us

profile of v4, /device:TPU:0, one launch (start us, length us, event | category | flops | bytes accessed | tf_op | source)
XLA Modules:
  0.0 66.5 jit_solution(4337880965389657230)
XLA Ops:
  1.3 59.9 %layer.1 = (bf16[256,2560]{1,0:T(8,128)(2,1)}, f32[40,256]{1,0:T(8,128)}, f32[1280,256]{1,0:T(8,128)}, f32[1,20]{1,0:T(1,128)}, f32[1,20]{1,0:T(1,128)}) custom-call(s32[1,1]{1,0:T(1,128)S(6)} %copy.18.tile, f32[40,256]{1,0:T(8,128)} %bitcast.14, f32[1,40]{1,0:T(1,128)} %bitcast.16, f32[1,40]{1,0:T(1,128)} %bitcast.17, bf16[256,2560]{1,0:T(8,128)(2,1)} %bitcast.11, ...), custom_call_target="tpu_custom_call" | custom-call | tf_op jit(solution)/shard_map/layer/pallas_call | solution.py:461
  61.2 0.0 copy-start.1
  61.2 0.0 copy-start
  61.2 2.6 %copy.19 = bf16[1,256,2560]{2,1,0:T(8,128)(2,1)} copy(bf16[1,256,2560]{2,1,0:T(8,128)(2,1)} %bitcast.10) | data formatting | bytes 2621440
  63.8 0.0 copy-done.1
  63.8 0.6 copy.20
  64.4 0.0 copy-done
  64.4 0.0 copy-start.3
  64.4 0.0 copy-start.2
  64.4 1.1 %copy.21 = f32[1280,256]{1,0:T(8,128)} copy(f32[1280,256]{1,0:T(8,128)S(1)} %copy-done) | data formatting | bytes 2621440
  65.5 0.0 copy-done.3
  65.5 0.5 copy.22
  66.0 0.0 copy-done.2
  66.0 0.5 copy.23
Async XLA Ops:
  61.2 2.6 %copy-start.1 = (f32[40,256]{1,0:T(8,128)S(1)}, f32[40,256]{1,0:T(8,128)}, u32[]{:S(2)}) copy-start(f32[40,256]{1,0:T(8,128)} %get-tuple-element.11) | copy-start | bytes 122884
  61.2 3.2 %copy-start = (f32[1280,256]{1,0:T(8,128)S(1)}, f32[1280,256]{1,0:T(8,128)}, u32[]{:S(2)}) copy-start(f32[1280,256]{1,0:T(8,128)} %get-tuple-element.22) | copy-start | bytes 3932164
  64.4 1.1 %copy-start.3 = (f32[1,20]{1,0:T(1,128)S(1)}, f32[1,20]{1,0:T(1,128)}, u32[]{:S(2)}) copy-start(f32[1,20]{1,0:T(1,128)} %get-tuple-element.13) | copy-start | bytes 244
  64.4 1.6 %copy-start.2 = (f32[1,20]{1,0:T(1,128)S(1)}, f32[1,20]{1,0:T(1,128)}, u32[]{:S(2)}) copy-start(f32[1,20]{1,0:T(1,128)} %get-tuple-element.14) | copy-start | bytes 244

commit v5 on v4

--- a/solution.py
+++ b/solution.py
@@ -465,7 +465,7 @@
         out_specs=(VMEM,) * 5,
         scratch_shapes=scratch,
         compiler_params=pltpu.CompilerParams(
-            collective_id=0, has_side_effects=True, vmem_limit_bytes=60 * 1024 * 1024
+            collective_id=0, has_side_effects=True, vmem_limit_bytes=58 * 1024 * 1024
         ),
         name="layer",
     )(

time: 66.7 us -> 66.7 us (level)
  no operation moved by 1% of the time
where the time goes in v5:
time: 66.7 us; the launch traced here: 66.5 us
  Pallas kernels  59.9 us (90%)
  local copies, waits for them, and re-layouts  5.27 us (8%)
  between operations  1.31 us (2%)
    pallas_call x1, Pallas kernels, shards(): pl.pallas_call(functools.partial(layer_kernel, bits, scenes, plans, chunk...  59.9 us
    unnamed x13, local copies, waits for them, and re-layouts  5.27 us

profile of v5, /device:TPU:0, one launch (start us, length us, event | category | flops | bytes accessed | tf_op | source)
XLA Modules:
  0.0 66.5 jit_solution(4337880965389657230)
XLA Ops:
  1.3 59.9 %layer.1 = (bf16[256,2560]{1,0:T(8,128)(2,1)}, f32[40,256]{1,0:T(8,128)}, f32[1280,256]{1,0:T(8,128)}, f32[1,20]{1,0:T(1,128)}, f32[1,20]{1,0:T(1,128)}) custom-call(s32[1,1]{1,0:T(1,128)S(6)} %copy.18.tile, f32[40,256]{1,0:T(8,128)} %bitcast.14, f32[1,40]{1,0:T(1,128)} %bitcast.16, f32[1,40]{1,0:T(1,128)} %bitcast.17, bf16[256,2560]{1,0:T(8,128)(2,1)} %bitcast.11, ...), custom_call_target="tpu_custom_call" | custom-call | tf_op jit(solution)/shard_map/layer/pallas_call | solution.py:461
  61.2 0.0 copy-start.1
  61.2 0.0 copy-start
  61.2 2.6 %copy.19 = bf16[1,256,2560]{2,1,0:T(8,128)(2,1)} copy(bf16[1,256,2560]{2,1,0:T(8,128)(2,1)} %bitcast.10) | data formatting | bytes 2621440
  63.8 0.0 copy-done.1
  63.8 0.6 copy.20
  64.4 0.0 copy-done
  64.4 0.0 copy-start.3
  64.4 0.0 copy-start.2
  64.4 1.1 %copy.21 = f32[1280,256]{1,0:T(8,128)} copy(f32[1280,256]{1,0:T(8,128)S(1)} %copy-done) | data formatting | bytes 2621440
  65.5 0.0 copy-done.3
  65.5 0.5 copy.22
  66.0 0.0 copy-done.2
  66.0 0.5 copy.23
Async XLA Ops:
  61.2 2.6 %copy-start.1 = (f32[40,256]{1,0:T(8,128)S(1)}, f32[40,256]{1,0:T(8,128)}, u32[]{:S(2)}) copy-start(f32[40,256]{1,0:T(8,128)} %get-tuple-element.11) | copy-start | bytes 122884
  61.2 3.2 %copy-start = (f32[1280,256]{1,0:T(8,128)S(1)}, f32[1280,256]{1,0:T(8,128)}, u32[]{:S(2)}) copy-start(f32[1280,256]{1,0:T(8,128)} %get-tuple-element.22) | copy-start | bytes 3932164
  64.4 1.1 %copy-start.3 = (f32[1,20]{1,0:T(1,128)S(1)}, f32[1,20]{1,0:T(1,128)}, u32[]{:S(2)}) copy-start(f32[1,20]{1,0:T(1,128)} %get-tuple-element.13) | copy-start | bytes 244
  64.4 1.6 %copy-start.2 = (f32[1,20]{1,0:T(1,128)S(1)}, f32[1,20]{1,0:T(1,128)}, u32[]{:S(2)}) copy-start(f32[1,20]{1,0:T(1,128)} %get-tuple-element.14) | copy-start | bytes 244
